TPU v7x, 32 devices: a whole 2x2x4 slice. The times are simulated.
32 devices in a mesh: seq: 8 (over z, y), tp: 4 (over x, core).
Axes of the slice: x: 2, y: 2, z: 4, core: 2. Of those that a mesh axis runs over, the one named last changes fastest.
Arguments:
- hidden_in: bfloat16 [4096, 2560], P('seq', 'tp'), may hold values from -24 to 24, as said below
- query_proj: bfloat16 [2560, 2048], P(None, 'tp'), may hold values from -0.125 to 0.125
- key_projection: bfloat16 [2560, 1024], P(None, 'tp'), may hold values from -0.125 to 0.125
- value_projection: bfloat16 [2560, 1024], P(None, 'tp'), may hold values from -0.125 to 0.125
- output_proj: bfloat16 [2048, 2560], P('tp'), may hold values from -0.125 to 0.125
- out_cotangent: bfloat16 [4096, 2560], P('seq', 'tp'), may hold values from -6 to 6
- doc_start: int32 [4096], P('seq'), may hold values from 0 to 4095, as said below
Outputs:
- hidden_grad: bfloat16 [4096, 2560], P('seq', 'tp')
- query_proj_grad: float32 [2560, 2048], P('seq', 'tp')
- key_proj_grad: float32 [2560, 1024], P('seq', 'tp')
- value_proj_grad: float32 [2560, 1024], P('seq', 'tp')
- output_proj_grad: float32 [2048, 2560], P('tp', 'seq')
Inputs may be any that keep to these rules, and one draw needn't show every extreme that they name: hidden_in's entries lie within the range. doc_start[0] = 0; doc_start[t] <= t; doc_start is constant within a document and equals t at each token t that begins one, so it never falls; the last token begins a document of its own.
All inputs are finite; a program needn't handle non-finite values.
Results may differ from a plain program's by a relative error of at most 0.035.
Values may be sent and summed in bfloat16 or wider, within the bound.
A program may use at most 128 MiB of HBM per device.

v0:
```python
from functools import partial
import math

import jax
import jax.numpy as jnp
from jax import lax
from jax.sharding import PartitionSpec as P

HEAD_SIZE = 256
LOOKBACK_SPAN = 1024


def from_behind(value, axis, steps):
    count = lax.axis_size(axis)
    first, last = (max(0, -steps), min(count, count - steps))
    return lax.ppermute(value, axis, [(source, source + steps) for source in range(first, last)])


def transposed_dot(left, right):
    return lax.dot_general(
        left, right, (((0,), (0,)), ((), ())), preferred_element_type=jnp.float32
    )


def right_transposed_dot(left, right):
    return lax.dot_general(
        left, right, (((1,), (1,)), ((), ())), preferred_element_type=jnp.float32
    )


def per_device(
    hidden_in, query_proj, key_projection, value_projection, output_proj, out_cotangent, doc_start
):
    tok_rows = hidden_in.shape[0]
    reach = LOOKBACK_SPAN // tok_rows
    my_index = lax.axis_index("seq")
    full_hidden, full_cotangent = (
        lax.all_gather(hidden_in, "tp", axis=1, tiled=True),
        lax.all_gather(out_cotangent, "tp", axis=1, tiled=True),
    )
    query_matrix = jnp.dot(full_hidden, query_proj, preferred_element_type=jnp.float32).astype(
        jnp.bfloat16
    )
    keys = jnp.dot(full_hidden, key_projection, preferred_element_type=jnp.float32).astype(
        jnp.bfloat16
    )
    values = jnp.dot(full_hidden, value_projection, preferred_element_type=jnp.float32).astype(
        jnp.bfloat16
    )
    attention_gradient = right_transposed_dot(full_cotangent, output_proj).astype(jnp.bfloat16)
    kv_heads = keys.shape[1] // HEAD_SIZE
    query_group = query_matrix.shape[1] // keys.shape[1]
    rows_of_query = query_matrix.reshape(tok_rows, kv_heads, query_group, HEAD_SIZE)
    gradient_rows = attention_gradient.reshape(tok_rows, kv_heads, query_group, HEAD_SIZE)
    key_blocks = [keys]
    value_blocks = [values]
    for offset in range(1, reach + 1):
        far_keys, far_values = from_behind((keys, values), "seq", offset)
        key_blocks.append(far_keys)
        value_blocks.append(far_values)
    local = jnp.arange(tok_rows, dtype=jnp.int32)
    q_pos = my_index * tok_rows + local
    scale = math.sqrt(HEAD_SIZE)

    def allowed_pairs(offset):
        k_pos = (my_index - offset) * tok_rows + local
        return (
            (k_pos[None, :] >= doc_start[:, None])
            & (k_pos[None, :] <= q_pos[:, None])
            & (q_pos[:, None] - k_pos[None, :] < LOOKBACK_SPAN)
        )

    def block_logits(offset):
        key_tile = key_blocks[offset].reshape(tok_rows, kv_heads, HEAD_SIZE)
        return (
            jnp.einsum(
                "ikgd,jkd->kgij", rows_of_query, key_tile, preferred_element_type=jnp.float32
            )
            / scale
        )

    def normalize(state, offset):
        running_max, running_sum = state
        masked = jnp.where(allowed_pairs(offset), block_logits(offset), -jnp.inf)
        new_max = jnp.maximum(running_max, jnp.max(masked, -1))
        running_sum = running_sum * jnp.exp(running_max - new_max) + jnp.sum(
            jnp.exp(masked - new_max[..., None]), -1
        )
        return (new_max, running_sum)

    state = (
        jnp.full((kv_heads, query_group, tok_rows), -jnp.inf, jnp.float32),
        jnp.zeros((kv_heads, query_group, tok_rows), jnp.float32),
    )
    for offset in range(reach + 1):
        step_fn = partial(normalize, offset=offset)
        state = step_fn(state)
    log_norm = state[0] + jnp.log(state[1])

    def block_probs(offset):
        return jnp.where(
            allowed_pairs(offset), jnp.exp(block_logits(offset) - log_norm[..., None]), 0.0
        )

    def attend(accum, offset):
        probability_reduced = block_probs(offset).astype(jnp.bfloat16)
        value_tile = value_blocks[offset].reshape(tok_rows, kv_heads, HEAD_SIZE)
        return accum + jnp.einsum(
            "kgij,jkd->ikgd", probability_reduced, value_tile, preferred_element_type=jnp.float32
        )

    attended = jnp.zeros((tok_rows, kv_heads, query_group, HEAD_SIZE), jnp.float32)
    for offset in range(reach + 1):
        step_fn = partial(attend, offset=offset)
        attended = step_fn(attended)
    attention_low = attended.astype(jnp.bfloat16)
    attention = attention_low.reshape(tok_rows, query_matrix.shape[1])
    output_proj_grad = lax.psum_scatter(
        transposed_dot(attention, full_cotangent).astype(jnp.bfloat16),
        "seq",
        scatter_dimension=1,
        tiled=True,
    ).astype(jnp.float32)
    delta = jnp.transpose(
        jnp.sum(gradient_rows.astype(jnp.float32) * attention_low.astype(jnp.float32), -1),
        (1, 2, 0),
    )

    def backward(accum, offset):
        probs = block_probs(offset)
        probability_reduced = probs.astype(jnp.bfloat16)
        key_tile = key_blocks[offset].reshape(tok_rows, kv_heads, HEAD_SIZE)
        value_tile = value_blocks[offset].reshape(tok_rows, kv_heads, HEAD_SIZE)
        prob_grad = jnp.einsum(
            "ikgd,jkd->kgij", gradient_rows, value_tile, preferred_element_type=jnp.float32
        )
        logit_gradient = (probs * (prob_grad - delta[..., None]) / scale).astype(jnp.bfloat16)
        accum = accum + jnp.einsum(
            "kgij,jkd->ikgd", logit_gradient, key_tile, preferred_element_type=jnp.float32
        )
        key_portion = jnp.einsum(
            "fqwc,wfqu->cfu", logit_gradient, rows_of_query, preferred_element_type=jnp.float32
        )
        value_portion = jnp.einsum(
            "fqwc,wfqu->cfu", probability_reduced, gradient_rows, preferred_element_type=jnp.float32
        )
        return (
            accum,
            key_portion.reshape(tok_rows, kv_heads * HEAD_SIZE),
            value_portion.reshape(tok_rows, kv_heads * HEAD_SIZE),
        )

    query_accum = jnp.zeros((tok_rows, kv_heads, query_group, HEAD_SIZE), jnp.float32)
    key_parts = []
    value_parts = []
    for offset in range(reach + 1):
        step_fn = partial(backward, offset=offset)
        query_accum, key_portion, value_portion = step_fn(query_accum)
        key_parts.append(key_portion)
        value_parts.append(value_portion)
    key_total = key_parts[0]
    value_total = value_parts[0]
    for offset in range(1, reach + 1):
        back_keys, back_values = from_behind(
            (key_parts[offset], value_parts[offset]), "seq", -offset
        )
        key_total = key_total + back_keys
        value_total = value_total + back_values
    query_grad = query_accum.reshape(tok_rows, query_matrix.shape[1]).astype(jnp.bfloat16)
    key_grad = key_total.astype(jnp.bfloat16)
    value_grad = value_total.astype(jnp.bfloat16)
    input_term = (
        right_transposed_dot(query_grad, query_proj)
        + right_transposed_dot(key_grad, key_projection)
        + right_transposed_dot(value_grad, value_projection)
    )
    hidden_grad = lax.psum_scatter(input_term, "tp", scatter_dimension=1, tiled=True).astype(
        jnp.bfloat16
    )
    query_proj_grad, key_proj_grad, value_proj_grad = (
        lax.psum_scatter(
            transposed_dot(full_hidden, query_grad).astype(jnp.bfloat16),
            "seq",
            scatter_dimension=0,
            tiled=True,
        ).astype(jnp.float32),
        lax.psum_scatter(
            transposed_dot(full_hidden, key_grad).astype(jnp.bfloat16),
            "seq",
            scatter_dimension=0,
            tiled=True,
        ).astype(jnp.float32),
        lax.psum_scatter(
            transposed_dot(full_hidden, value_grad).astype(jnp.bfloat16),
            "seq",
            scatter_dimension=0,
            tiled=True,
        ).astype(jnp.float32),
    )
    return (hidden_grad, query_proj_grad, key_proj_grad, value_proj_grad, output_proj_grad)


def solution(mesh):
    placed = (
        P("seq", "tp"),
        P(None, "tp"),
        P(None, "tp"),
        P(None, "tp"),
        P("tp", None),
        P("seq", "tp"),
        P("seq"),
    )
    return jax.shard_map(
        per_device,
        mesh=mesh,
        in_specs=placed,
        out_specs=(P("seq", "tp"), P("seq", "tp"), P("seq", "tp"), P("seq", "tp"), P("tp", "seq")),
        check_vma=False,
    )
```

profile of v0, /device:TPU:0, one launch (start us, length us, event | category | flops | bytes accessed | tf_op | source)
XLA Modules:
  0.0 458.5 jit_solution(3666904262897598273)
XLA Ops:
  8.8 2.4 fusion.40
  11.2 26.7 %all-gather.3.cloned.1.call-done = bf16[512,2560]{1,0:T(8,128)(2,1)} async-done(((bf16[512,640]{1,0:T(8,128)(2,1)}), bf16[512,2560]{1,0:T(8,128)(2,1)}) %all-gather.3.cloned.1.call-update) | async-done | bytes 2621456 | tf_op jit(solution)/shard_map/all_gather | solution.py:38
  37.9 3.8 convolution_convert_fusion.7
  41.7 4.1 collective-permute-start.1
  45.8 4.1 collective-permute-start
  49.9 1.6 convolution_convert_fusion.6
  51.4 2.7 collective-permute-start.2
  54.1 3.4 collective-permute-start.3
  57.5 1.6 convolution_convert_fusion.5
  59.1 5.9 %all-gather.5.cloned.1.call-done = bf16[512,2560]{1,0:T(8,128)(2,1)} async-done(((bf16[512,640]{1,0:T(8,128)(2,1)}), bf16[512,2560]{1,0:T(8,128)(2,1)}) %all-gather.5.cloned.1.call-update) | async-done | bytes 2621456 | tf_op jit(solution)/shard_map/all_gather | solution.py:39
  65.0 4.1 convolution_convert_fusion.4
  69.1 1.7 fusion.18
  71.4 1.7 fusion.19
  73.1 1.7 fusion.20
  75.9 1.7 fusion.46
  77.5 1.7 convolution_add_fusion.3
  79.2 2.5 fusion.38
  81.7 1.9 fusion.26
  85.0 1.9 fusion.25
  87.4 1.3 collective-permute-start.4
  88.7 1.5 collective-permute-start.5
  90.2 1.9 fusion.24
  92.1 11.2 %collective-permute-done.4 = f32[512,256]{0,1:T(8,128)S(1)} collective-permute-done((f32[512,256]{0,1:T(8,128)S(1)}, f32[512,256]{0,1:T(8,128)S(1)}, u32[]{:S(2)}, u32[]{:S(2)}) %collective-permute-start.4) | collective-permute-done | bytes 524320 | tf_op jit(solution)/shard_map/ppermute | solution.py:16
  103.4 12.1 %collective-permute-done.5 = f32[512,256]{0,1:T(8,128)S(1)} collective-permute-done((f32[512,256]{0,1:T(8,128)S(1)}, f32[512,256]{0,1:T(8,128)S(1)}, u32[]{:S(2)}, u32[]{:S(2)}) %collective-permute-start.5) | collective-permute-done | bytes 524320 | tf_op jit(solution)/shard_map/ppermute | solution.py:16
  116.0 1.9 fusion.1
  117.9 2.5 copy.98
  120.5 2.6 convolution_bitcast_fusion
  124.0 1.4 collective-permute-start.6
  125.4 1.3 collective-permute-start.7
  126.7 15.8 %collective-permute-done.6 = f32[512,256]{0,1:T(8,128)S(1)} collective-permute-done((f32[512,256]{0,1:T(8,128)S(1)}, f32[512,256]{0,1:T(8,128)S(1)}, u32[]{:S(2)}, u32[]{:S(2)}) %collective-permute-start.6) | collective-permute-done | bytes 524320 | tf_op jit(solution)/shard_map/ppermute | solution.py:16
  142.5 18.3 %collective-permute-done.7 = f32[512,256]{0,1:T(8,128)S(1)} collective-permute-done((f32[512,256]{0,1:T(8,128)S(1)}, f32[512,256]{0,1:T(8,128)S(1)}, u32[]{:S(2)}, u32[]{:S(2)}) %collective-permute-start.7) | collective-permute-done | bytes 524320 | tf_op jit(solution)/shard_map/ppermute | solution.py:16
  162.2 1.9 fusion.2
  164.2 2.4 copy.100
  166.7 1.8 fusion.57
  168.6 1.5 convolution_add_fusion.1
  170.1 1.6 fusion.28
  172.0 3.1 fusion
  175.1 4.4 copy.96
  179.6 5.1 %convolution_convert_fusion = bf16[512,2560]{0,1:T(8,128)(2,1)} fusion(bf16[512,512]{0,1:T(8,128)(2,1)} %bitcast.309, bf16[512,2560]{1,0:T(8,128)(2,1)} %all-gather.5.cloned.1.call-done), kind=kOutput, calls=%fused_computation.1 | convolution fusion | flops 1343488000 | bytes 5767168 | tf_op jit(solution)/shard_map/dot_general | solution.py:20
  185.0 1.6 fusion.66
  187.9 3.2 add_add_fusion
  193.2 57.9 %reduce-scatter.20.cloned.1.call-done = bf16[320,256]{1,0:T(8,128)(2,1)} async-done(((bf16[2560,256]{1,0:T(8,128)(2,1)}), bf16[320,256]{1,0:T(8,128)(2,1)}) %reduce-scatter.20.cloned.1.call-update) | async-done | bytes 163856
  253.0 70.8 %reduce-scatter.16.cloned.1.call-done = bf16[320,512]{1,0:T(8,128)(2,1)} async-done(((bf16[2560,512]{1,0:T(8,128)(2,1)}), bf16[320,512]{1,0:T(8,128)(2,1)}) %reduce-scatter.16.cloned.1.call-update) | async-done | bytes 327696
  323.9 1.2 copy.97
  326.1 70.5 %reduce-scatter.14.cloned.1.call-done = bf16[512,320]{0,1:T(8,128)(2,1)} async-done(((bf16[512,2560]{0,1:T(8,128)(2,1)}), bf16[512,320]{0,1:T(8,128)(2,1)}) %reduce-scatter.14.cloned.1.call-update) | async-done | bytes 327696 | tf_op jit(solution)/shard_map/reduce_scatter | solution.py:118
  396.6 1.9 convert_element_type.146
  398.5 51.0 %reduce-scatter.12.cloned.1.call-done = f32[512,640]{1,0:T(8,128)} async-done(((f32[512,2560]{1,0:T(8,128)}), f32[512,640]{1,0:T(8,128)}) %reduce-scatter.12.cloned.1.call-update) | async-done | bytes 1310736 | tf_op jit(solution)/shard_map/reduce_scatter | solution.py:177
  449.4 2.2 convert_element_type.135
  (93 shorter events, 14.8 us)
Async XLA Ops:
  7.2 50.3 %copy-start = (bf16[2560,512]{1,0:T(8,128)(2,1)S(1)}, bf16[2560,512]{1,0:T(8,128)(2,1)}, u32[]{:S(2)}) copy-start(bf16[2560,512]{1,0:T(8,128)(2,1)} %param.8) | copy-start | bytes 7864324
  7.2 30.7 %all-gather.3.cloned.1.call-start = ((), (), s32[]{:S(2)}) async-start(), calls=%async_computation.5 | async-start | bytes 3276800 | tf_op jit(solution)/shard_map/all_gather | solution.py:38
  7.9 57.1 %all-gather.5.cloned.1.call-start = ((), (), s32[]{:S(2)}) async-start(), calls=%async_computation.6 | async-start | bytes 3276800 | tf_op jit(solution)/shard_map/all_gather | solution.py:39
  8.7 182.6 %reduce-scatter.18.cloned.1.call-start = ((), (), s32[]{:S(2)}) async-start(), calls=%async_computation.10 | async-start | bytes 1474560
  11.2 73.8 %copy-start.12 = (pred[512,512]{0,1:T(8,128)(4,1)}, pred[512,512]{0,1:T(8,128)(4,1)S(1)}, u32[]{:S(2)}) copy-start(pred[512,512]{0,1:T(8,128)(4,1)S(1)} %get-tuple-element.17) | copy-start | bytes 786436
  37.8 12.0 %copy-start.1 = (bf16[512,2560]{1,0:T(8,128)(2,1)S(1)}, bf16[512,2560]{1,0:T(8,128)(2,1)}, u32[]{:S(2)}) copy-start(bf16[512,2560]{1,0:T(8,128)(2,1)} %all-gather.3.cloned.1.call-done) | copy-start | bytes 7864324
  37.8 12.0 %copy-start.17 = (bf16[2560,256]{1,0:T(8,128)(2,1)S(1)}, bf16[2560,256]{1,0:T(8,128)(2,1)}, u32[]{:S(2)}) copy-start(bf16[2560,256]{1,0:T(8,128)(2,1)} %param.10) | copy-start | bytes 3932164
  41.7 31.5 %collective-permute-start.1 = (bf16[512,256]{1,0:T(8,128)(2,1)}, bf16[512,256]{1,0:T(8,128)(2,1)}, u32[]{:S(2)}, u32[]{:S(2)}) collective-permute-start(bf16[512,256]{1,0:T(8,128)(2,1)} %convolution_convert_fusion.7), channel_id=1, source_target_pairs={{0,8},{4,12},{8,16},{12,20},{16,24},{20,28},{1,9},{5,13},{9,17},{1... | collective-permute-start | bytes 786440 | tf_op jit(solution)/shard_map/ppermute | solution.py:16
  45.8 25.6 %collective-permute-start = (bf16[512,256]{1,0:T(8,128)(2,1)}, bf16[512,256]{1,0:T(8,128)(2,1)}, u32[]{:S(2)}, u32[]{:S(2)}) collective-permute-start(bf16[512,256]{1,0:T(8,128)(2,1)} %convolution_convert_fusion.7), channel_id=1, source_target_pairs={{0,4},{4,8},{8,12},{12,16},{16,20},{20,24},{24,28},{1,5},{5,9},{9,... | collective-permute-start | bytes 786440 | tf_op jit(solution)/shard_map/ppermute | solution.py:16
  51.4 26.1 %collective-permute-start.2 = (bf16[512,256]{1,0:T(8,128)(2,1)}, bf16[512,256]{1,0:T(8,128)(2,1)}, u32[]{:S(2)}, u32[]{:S(2)}) collective-permute-start(bf16[512,256]{1,0:T(8,128)(2,1)} %convolution_convert_fusion.6), channel_id=1, source_target_pairs={{0,4},{4,8},{8,12},{12,16},{16,20},{20,24},{24,28},{1,5},{5,9},{9,... | collective-permute-start | bytes 786440 | tf_op jit(solution)/shard_map/ppermute | solution.py:16
  54.1 25.1 %collective-permute-start.3 = (bf16[512,256]{1,0:T(8,128)(2,1)}, bf16[512,256]{1,0:T(8,128)(2,1)}, u32[]{:S(2)}, u32[]{:S(2)}) collective-permute-start(bf16[512,256]{1,0:T(8,128)(2,1)} %convolution_convert_fusion.6), channel_id=1, source_target_pairs={{0,8},{4,12},{8,16},{12,20},{16,24},{20,28},{1,9},{5,13},{9,17},{1... | collective-permute-start | bytes 786440 | tf_op jit(solution)/shard_map/ppermute | solution.py:16
  65.0 4.1 copy-start.22
  69.1 21.1 %copy-start.26 = (bf16[512,512]{0,1:T(8,128)(2,1)}, bf16[512,512]{0,1:T(8,128)(2,1)S(1)}, u32[]{:S(2)}) copy-start(bf16[512,512]{0,1:T(8,128)(2,1)S(1)} %convolution_convert_fusion.4) | copy-start | bytes 1572868
  70.8 19.4 %copy-start.14 = (f32[512,512,2]{1,0,2:T(8,128)}, f32[512,512,2]{1,0,2:T(8,128)S(1)}, u32[]{:S(2)}) copy-start(f32[512,512,2]{1,0,2:T(8,128)S(1)} %get-tuple-element.23) | copy-start | bytes 6291460
  71.3 1.8 copy-start.24
  73.1 11.9 %copy-start.5 = (f32[512,512,2]{1,0,2:T(8,128)}, f32[512,512,2]{1,0,2:T(8,128)S(1)}, u32[]{:S(2)}) copy-start(f32[512,512,2]{1,0,2:T(8,128)S(1)} %get-tuple-element.25) | copy-start | bytes 6291460
  74.8 6.9 %copy-start.16 = (f32[512,512,2]{1,0,2:T(8,128)}, f32[512,512,2]{1,0,2:T(8,128)S(1)}, u32[]{:S(2)}) copy-start(f32[512,512,2]{1,0,2:T(8,128)S(1)} %get-tuple-element.21) | copy-start | bytes 6291460
  83.6 1.0 copy-start.9
  86.9 3.3 copy-start.7
  87.4 16.0 %collective-permute-start.4 = (f32[512,256]{0,1:T(8,128)S(1)}, f32[512,256]{0,1:T(8,128)S(1)}, u32[]{:S(2)}, u32[]{:S(2)}) collective-permute-start(f32[512,256]{0,1:T(8,128)S(1)} %convolution_bitcast_fusion.4), channel_id=1, source_target_pairs={{4,0},{8,4},{12,8},{16,12},{20,16},{24,20},{28,24},{5,1},{9,5},{13... | collective-permute-start | bytes 1572872 | tf_op jit(solution)/shard_map/ppermute | solution.py:16
  88.7 26.8 %collective-permute-start.5 = (f32[512,256]{0,1:T(8,128)S(1)}, f32[512,256]{0,1:T(8,128)S(1)}, u32[]{:S(2)}, u32[]{:S(2)}) collective-permute-start(f32[512,256]{0,1:T(8,128)S(1)} %convolution_bitcast_fusion.3), channel_id=1, source_target_pairs={{8,0},{12,4},{16,8},{20,12},{24,16},{28,20},{9,1},{13,5},{17,9},{2... | collective-permute-start | bytes 1572872 | tf_op jit(solution)/shard_map/ppermute | solution.py:16
  92.1 23.9 %copy-start.11 = (bf16[2,512,512]{1,2,0:T(8,128)(2,1)}, bf16[2,512,512]{1,2,0:T(8,128)(2,1)S(1)}, u32[]{:S(2)}) copy-start(bf16[2,512,512]{1,2,0:T(8,128)(2,1)S(1)} %fusion.24) | copy-start | bytes 3145732
  92.1 23.9 %copy-start.2 = (bf16[512,2560]{1,0:T(8,128)(2,1)S(1)}, bf16[512,2560]{1,0:T(8,128)(2,1)}, u32[]{:S(2)}) copy-start(bf16[512,2560]{1,0:T(8,128)(2,1)} %all-gather.3.cloned.1.call-done) | copy-start | bytes 7864324
  117.9 2.6 copy-start.25
  120.5 2.7 copy-start.13
  120.5 130.6 %reduce-scatter.20.cloned.1.call-start = ((), (), s32[]{:S(2)}) async-start(), calls=%async_computation.11 | async-start | bytes 1474560
  120.5 2.7 copy-start.6
  120.5 2.7 copy-start.27
  123.2 37.6 %copy-start.15 = (f32[512,512,2]{1,0,2:T(8,128)S(1)}, f32[512,512,2]{1,0,2:T(8,128)}, u32[]{:S(2)}) copy-start(f32[512,512,2]{1,0,2:T(8,128)} %copy-done.14) | copy-start | bytes 6291460
  123.2 37.6 %copy-start.23 = (pred[512,512]{0,1:T(8,128)(4,1)S(1)}, pred[512,512]{0,1:T(8,128)(4,1)}, u32[]{:S(2)}) copy-start(pred[512,512]{0,1:T(8,128)(4,1)} %get-tuple-element.19) | copy-start | bytes 786436
  124.0 38.3 %copy-start.3 = (bf16[512,2560]{1,0:T(8,128)(2,1)S(1)}, bf16[512,2560]{1,0:T(8,128)(2,1)}, u32[]{:S(2)}) copy-start(bf16[512,2560]{1,0:T(8,128)(2,1)} %all-gather.3.cloned.1.call-done) | copy-start | bytes 7864324
  124.0 18.5 %collective-permute-start.6 = (f32[512,256]{0,1:T(8,128)S(1)}, f32[512,256]{0,1:T(8,128)S(1)}, u32[]{:S(2)}, u32[]{:S(2)}) collective-permute-start(f32[512,256]{0,1:T(8,128)S(1)} %convolution_bitcast_fusion.1), channel_id=1, source_target_pairs={{4,0},{8,4},{12,8},{16,12},{20,16},{24,20},{28,24},{5,1},{9,5},{13... | collective-permute-start | bytes 1572872 | tf_op jit(solution)/shard_map/ppermute | solution.py:16
  125.4 35.4 %collective-permute-start.7 = (f32[512,256]{0,1:T(8,128)S(1)}, f32[512,256]{0,1:T(8,128)S(1)}, u32[]{:S(2)}, u32[]{:S(2)}) collective-permute-start(f32[512,256]{0,1:T(8,128)S(1)} %convolution_bitcast_fusion), channel_id=1, source_target_pairs={{8,0},{12,4},{16,8},{20,12},{24,16},{28,20},{9,1},{13,5},{17,9},{2... | collective-permute-start | bytes 1572872 | tf_op jit(solution)/shard_map/ppermute | solution.py:16
  161.5 0.7 copy-start.20
  166.6 157.3 %reduce-scatter.16.cloned.1.call-start = ((), (), s32[]{:S(2)}) async-start(), calls=%async_computation.9 | async-start | bytes 2949120
  166.7 1.9 copy-start.8
  168.5 1.5 copy-start.10
  170.1 1.9 copy-start.4
  179.5 217.1 %reduce-scatter.14.cloned.1.call-start = ((), (), s32[]{:S(2)}) async-start(), calls=%async_computation.8 | async-start | bytes 2949120 | tf_op jit(solution)/shard_map/reduce_scatter | solution.py:118
  184.7 264.7 %reduce-scatter.12.cloned.1.call-start = ((), (), s32[]{:S(2)}) async-start(), calls=%async_computation.7 | async-start | bytes 6553600 | tf_op jit(solution)/shard_map/reduce_scatter | solution.py:177
  185.0 1.6 copy-start.19
  186.6 1.3 copy-start.18
  186.6 1.3 copy-start.21
Sparse Core Ops, SparseCore 0:
  9.6 28.2 all-gather.2
  39.4 25.5 all-gather.4
  120.6 63.8 reduce-scatter.17
  187.7 63.3 reduce-scatter.19
  254.5 69.3 reduce-scatter.15
  327.2 69.2 reduce-scatter.13
  399.1 50.2 reduce-scatter.11
where the time goes:
time: 459 us
  waiting for transfers between devices  342 us (75%)
  matrix products  55.7 us (12%)
  starting transfers between devices  20.3 us (4%)
  local copies, waits for them, and re-layouts  18 us (4%)
  between operations  14.7 us (3%)
  other arithmetic  8.07 us (2%)
    unnamed x10, waiting for transfers between devices  130 us
    reduce_scatter x1, waiting for transfers between devices, per_device(): lax.psum_scatter(transposed_dot(attention, full_cotangent).astype(jnp.bfl...  70.5 us
    ppermute x8, waiting for transfers between devices, from_behind(): lax.ppermute(value, axis, [(source, source + steps) for source in range(f...  57.5 us
    reduce_scatter x1, waiting for transfers between devices, per_device(): lax.psum_scatter(input_term, 'tp', scatter_dimension=1, tiled=True)  51 us
    all_gather x1, waiting for transfers between devices, per_device(): lax.all_gather(hidden_in, 'tp', axis=1, tiled=True)  26.7 us
    ppermute x8, starting transfers between devices, from_behind(): lax.ppermute(value, axis, [(source, source + steps) for source in range(f...  19.8 us
    unnamed x65, local copies, waits for them, and re-layouts  18 us
    dot_general x4, matrix products, transposed_dot(): lax.dot_general(left, right, (((0,), (0,)), ((), ())), preferred_element_...  12 us
  transfers between devices with their start and end apart: 15, of which 10 were waited for; matrix products, arithmetic and copies ran while one was open for 14% of the time, Pallas kernels for 0%

commit v1 on v0

v1 whole, which is shorter than its diff:
```python
import math

import jax
import jax.numpy as jnp
from jax import lax
from jax.sharding import PartitionSpec as P

HEAD_SIZE = 256
LOOKBACK_SPAN = 1024
BF16 = jnp.bfloat16
F32 = jnp.float32


def dot(left, right):
    return jnp.dot(left, right, preferred_element_type=F32)


def transposed_dot(left, right):
    return lax.dot_general(left, right, (((0,), (0,)), ((), ())), preferred_element_type=F32)


def right_transposed_dot(left, right):
    return lax.dot_general(left, right, (((1,), (1,)), ((), ())), preferred_element_type=F32)


def swap(value, axis, bit):
    count = lax.axis_size(axis)
    return lax.ppermute(value, axis, [(i, i ^ bit) for i in range(count)])


def shift(value, steps):
    count = lax.axis_size("seq")
    return lax.ppermute(
        value, "seq", [(i, i + steps) for i in range(count) if 0 <= i + steps < count]
    )


def gather_features(block):
    me = lax.axis_index("tp")
    high, low = me // 2, me % 2
    other = swap(block, "tp", 2)
    first = jnp.where(high == 0, block, other)
    second = jnp.where(high == 0, other, block)
    near_first, near_second = swap(first, "tp", 1), swap(second, "tp", 1)
    return jnp.concatenate(
        [
            jnp.where(low == 0, first, near_first),
            jnp.where(low == 0, near_first, first),
            jnp.where(low == 0, second, near_second),
            jnp.where(low == 0, near_second, second),
        ],
        axis=1,
    )


def chain_sum(parts):
    levels = parts.shape[0]
    level = lax.axis_index("seq") // 2
    up = down = None

    def block(index):
        return lax.dynamic_index_in_dim(parts, jnp.clip(index, 0, levels - 1), 0, keepdims=False)

    def added(value, arrived):
        if arrived is None:
            return value
        return (value.astype(F32) + arrived.astype(F32)).astype(BF16)

    for step in range(levels - 1):
        gap = levels - 1 - step
        up_value = added(block(level + gap), up)
        down_value = added(block(level - gap), down)
        ups, downs = [], []
        for z in range(levels):
            for y in range(2):
                if z <= step:
                    ups.append((2 * z + y, 2 * z + 2 + y))
                if z >= gap:
                    downs.append((2 * z + y, 2 * z - 2 + y))
        up = lax.ppermute(up_value, "seq", ups)
        down = lax.ppermute(down_value, "seq", downs)
    total = block(level).astype(F32)
    if up is not None:
        total = total + up.astype(F32) + down.astype(F32)
    return total


def per_device(
    hidden_in, query_proj, key_projection, value_projection, output_proj, out_cotangent, doc_start
):
    tok_rows, shard_width = hidden_in.shape
    reach = LOOKBACK_SPAN // tok_rows
    seq_count = lax.axis_size("seq")
    tp_count = lax.axis_size("tp")
    levels = seq_count // 2
    my_index = lax.axis_index("seq")
    parity = my_index % 2
    width = shard_width * tp_count
    piece = width // seq_count

    def halves(array):
        split = array.reshape(tok_rows, -1, 2, piece)
        even = split[:, :, 0].reshape(tok_rows, -1)
        odd = split[:, :, 1].reshape(tok_rows, -1)
        mine = jnp.where(parity == 0, even, odd)
        theirs = jnp.where(parity == 0, odd, even)
        return mine, theirs

    full_hidden = gather_features(hidden_in)
    key_values = dot(full_hidden, jnp.concatenate([key_projection, value_projection], 1)).astype(BF16)
    halo = [shift(key_values, offset) for offset in range(1, reach + 1)]
    full_cotangent = gather_features(out_cotangent)
    query_matrix = dot(full_hidden, query_proj).astype(BF16)
    attention_gradient = right_transposed_dot(full_cotangent, output_proj).astype(BF16)

    hidden_theirs = swap(halves(hidden_in)[1], "seq", 1)
    cot_theirs = swap(halves(out_cotangent)[1], "seq", 1)
    hidden_pair = jnp.concatenate(
        [halves(full_hidden)[0], gather_features(hidden_theirs)], 0
    )
    cot_pair = jnp.concatenate([halves(full_cotangent)[0], gather_features(cot_theirs)], 0)

    kv_width = key_projection.shape[1]
    kv_heads = kv_width // HEAD_SIZE
    group = query_proj.shape[1] // kv_width
    span = (reach + 1) * tok_rows
    window = jnp.concatenate(halo[::-1] + [key_values], 0)
    scale = math.sqrt(HEAD_SIZE)
    q_pos = my_index * tok_rows + jnp.arange(tok_rows, dtype=jnp.int32)
    k_pos = (my_index - reach) * tok_rows + jnp.arange(span, dtype=jnp.int32)
    allowed = (
        (k_pos[None, :] >= doc_start[:, None])
        & (k_pos[None, :] <= q_pos[:, None])
        & (q_pos[:, None] - k_pos[None, :] < LOOKBACK_SPAN)
    )
    attention, query_grad, key_parts, value_parts = [], [], [], []
    for kv in range(kv_heads):
        keys = window[:, kv * HEAD_SIZE : (kv + 1) * HEAD_SIZE]
        values = window[:, kv_width + kv * HEAD_SIZE : kv_width + (kv + 1) * HEAD_SIZE]
        key_total = value_total = 0.0
        for member in range(group):
            at = (kv * group + member) * HEAD_SIZE
            queries = query_matrix[:, at : at + HEAD_SIZE]
            grads = attention_gradient[:, at : at + HEAD_SIZE]
            logits = jnp.where(allowed, right_transposed_dot(queries, keys) / scale, -jnp.inf)
            weights = jnp.exp(logits - jnp.max(logits, -1, keepdims=True))
            probs = weights * (1.0 / jnp.sum(weights, -1, keepdims=True))
            probs_low = probs.astype(BF16)
            attended = dot(probs_low, values).astype(BF16)
            delta = jnp.sum(grads.astype(F32) * attended.astype(F32), -1, keepdims=True)
            prob_grad = right_transposed_dot(grads, values)
            logit_grad = (probs * (prob_grad - delta) / scale).astype(BF16)
            attention.append(attended)
            query_grad.append(dot(logit_grad, keys).astype(BF16))
            key_total = key_total + transposed_dot(logit_grad, queries)
            value_total = value_total + transposed_dot(probs_low, grads)
        key_parts.append(key_total)
        value_parts.append(value_total)
    attention = jnp.concatenate(attention, 1)
    query_grad = jnp.concatenate(query_grad, 1)
    parts = jnp.concatenate(key_parts + value_parts, 1)
    kv_total = parts[reach * tok_rows :]
    for offset in range(1, reach + 1):
        start = (reach - offset) * tok_rows
        kv_total = kv_total + shift(
            parts[start : start + tok_rows].astype(BF16), -offset
        ).astype(F32)
    kv_grad = kv_total.astype(BF16)

    attention_pair = jnp.concatenate([attention, swap(attention, "seq", 1)], 0)
    query_pair = jnp.concatenate([query_grad, swap(query_grad, "seq", 1)], 0)
    kv_pair = jnp.concatenate([kv_grad, swap(kv_grad, "seq", 1)], 0)

    def summed(left, right):
        return chain_sum(
            transposed_dot(left, right).astype(BF16).reshape(levels, piece, right.shape[1])
        )

    output_proj_grad = summed(cot_pair, attention_pair).T
    query_proj_grad = summed(hidden_pair, query_pair)
    kv_proj_grad = summed(hidden_pair, kv_pair)

    term = (
        right_transposed_dot(query_grad, query_proj)
        + right_transposed_dot(kv_grad[:, :kv_width], key_projection)
        + right_transposed_dot(kv_grad[:, kv_width:], value_projection)
    ).astype(BF16)
    me = lax.axis_index("tp")
    blocks = [term[:, i * shard_width : (i + 1) * shard_width] for i in range(tp_count)]
    high, low = me // 2, me % 2
    near = [
        jnp.where(low == 0, blocks[2 * i], blocks[2 * i + 1]).astype(F32)
        + swap(jnp.where(low == 0, blocks[2 * i + 1], blocks[2 * i]), "tp", 1).astype(F32)
        for i in range(2)
    ]
    far = swap(jnp.where(high == 0, near[1], near[0]).astype(BF16), "tp", 2)
    hidden_grad = (jnp.where(high == 0, near[0], near[1]) + far.astype(F32)).astype(BF16)
    return (
        hidden_grad,
        query_proj_grad,
        kv_proj_grad[:, :kv_width],
        kv_proj_grad[:, kv_width:],
        output_proj_grad,
    )


def solution(mesh):
    placed = (
        P("seq", "tp"),
        P(None, "tp"),
        P(None, "tp"),
        P(None, "tp"),
        P("tp", None),
        P("seq", "tp"),
        P("seq"),
    )
    return jax.shard_map(
        per_device,
        mesh=mesh,
        in_specs=placed,
        out_specs=(P("seq", "tp"), P("seq", "tp"), P("seq", "tp"), P("seq", "tp"), P("tp", "seq")),
        check_vma=False,
    )
```

time: 459 us -> 247 us (0.54)
  waiting for transfers between devices: 342 us -> 99.6 us
  starting transfers between devices: 20.3 us -> 67.8 us
  matrix products: 55.7 us -> 26.3 us
  other arithmetic: 8.07 us -> 31.8 us
  between operations: 14.7 us -> 1.57 us
    unnamed x10 -> x0, waiting for transfers between devices: 130 us -> none
    reduce_scatter x2 -> x0, waiting for transfers between devices: 121 us -> none  [the longest x1 70.5 us: per_device(): lax.psum_scatter(transposed_dot(attention, full_cotangent).astype(jnp.bfl...]
    ppermute x8 -> x42, starting transfers between devices: 19.8 us -> 67.8 us  [the longest x9 34.7 us: chain_sum(): up = lax.ppermute(up_value, 'seq', ups)]
    ppermute x8 -> x42, waiting for transfers between devices: 57.5 us -> 99.6 us  [the longest x20 61.1 us: swap(): return lax.ppermute(value, axis, [(i, i ^ bit) for i in range(count)])]
    all_gather x2 -> x0, waiting for transfers between devices: 32.6 us -> none  [the longest x1 26.7 us: per_device(): lax.all_gather(hidden_in, 'tp', axis=1, tiled=True)]
    dot_general x21 -> x6, matrix products: 33.8 us -> 7.29 us  [dot(): return jnp.dot(left, right, preferred_element_type=F32)]
    select_n x0 -> x17, other arithmetic: none -> 19.1 us  [the longest x4 5.71 us: gather_features(): first = jnp.where(high == 0, block, other)]
    unnamed x65 -> x64, local copies, waits for them, and re-layouts: 18 us -> 6.72 us
  transfers between devices with their start and end apart: 15 -> 42, of which waited for: 10 -> 13; matrix products, arithmetic and copies ran while one was open for 14% -> 22% of each run, Pallas kernels for 0% -> 0%
where the time goes in v1:
time: 247 us; the launch traced here: 244 us
  waiting for transfers between devices  99.6 us (40%)
  starting transfers between devices  67.8 us (27%)
  other arithmetic  31.8 us (13%)
  matrix products  26.3 us (11%)
  local copies, waits for them, and re-layouts  16.6 us (7%)
    ppermute x20, waiting for transfers between devices, swap(): return lax.ppermute(value, axis, [(i, i ^ bit) for i in range(count)])  61.1 us
    ppermute x9, starting transfers between devices, chain_sum(): up = lax.ppermute(up_value, 'seq', ups)  34.7 us
    ppermute x9, waiting for transfers between devices, chain_sum(): up = lax.ppermute(up_value, 'seq', ups)  16.7 us
    ppermute x9, waiting for transfers between devices, chain_sum(): down = lax.ppermute(down_value, 'seq', downs)  16.3 us
    ppermute x20, starting transfers between devices, swap(): return lax.ppermute(value, axis, [(i, i ^ bit) for i in range(count)])  14.9 us
    dot_general x8, matrix products, right_transposed_dot(): lax.dot_general(left, right, (((1,), (1,)), ((), ())), preferred_element_...  11.7 us
    ppermute x4, starting transfers between devices, shift(): lax.ppermute(value, 'seq', [(i, i + steps) for i in range(count) if 0 <=...  10.3 us
    concatenate x2, local copies, waits for them, and re-layouts, gather_features(): jnp.concatenate([jnp.where(low == 0, first, near_first), jnp.where(low ==...  8.8 us
  transfers between devices with their start and end apart: 42, of which 13 were waited for; matrix products, arithmetic and copies ran while one was open for 22% of the time, Pallas kernels for 0%

profile of v1, /device:TPU:0, one launch (start us, length us, event | category | flops | bytes accessed | tf_op | source)
XLA Modules:
  0.0 243.6 jit_solution(5270778875950650509)
XLA Ops:
  0.7 1.5 copy.16
  2.9 3.0 %collective-permute-start.13 = (bf16[512,320]{0,1:T(8,128)(2,1)}, bf16[512,320]{0,1:T(8,128)(2,1)}, u32[]{:S(2)}, u32[]{:S(2)}) collective-permute-start(bf16[512,320]{0,1:T(8,128)(2,1)} %fusion.70), channel_id=1, source_target_pairs={{0,4},{4,0},{8,12},{12,8},{16,20},{20,16},{24,28},{28,24},{1,5},{5... | collective-permute-start | bytes 983048 | tf_op jit(solution)/shard_map/ppermute | solution.py:28
  8.0 6.7 %collective-permute-done.13 = bf16[512,320]{0,1:T(8,128)(2,1)} collective-permute-done((bf16[512,320]{0,1:T(8,128)(2,1)}, bf16[512,320]{0,1:T(8,128)(2,1)}, u32[]{:S(2)}, u32[]{:S(2)}) %collective-permute-start.13) | collective-permute-done | bytes 327712 | tf_op jit(solution)/shard_map/ppermute | solution.py:28
  14.7 2.0 collective-permute-start.14
  16.8 2.0 collective-permute-start.5
  18.8 2.1 collective-permute-done.31
  20.9 1.7 collective-permute-start.32
  22.6 3.1 %collective-permute-done.14 = bf16[512,320]{0,1:T(8,128)(2,1)} collective-permute-done((bf16[512,320]{0,1:T(8,128)(2,1)}, bf16[512,320]{0,1:T(8,128)(2,1)}, u32[]{:S(2)}, u32[]{:S(2)}) %collective-permute-start.14) | collective-permute-done | bytes 327712 | tf_op jit(solution)/shard_map/ppermute | solution.py:28
  27.4 30.7 %collective-permute-done.32 = bf16[512,320]{0,1:T(8,128)(2,1)S(1)} collective-permute-done((bf16[512,320]{0,1:T(8,128)(2,1)}, bf16[512,320]{0,1:T(8,128)(2,1)S(1)}, u32[]{:S(2)}, u32[]{:S(2)}) %collective-permute-start.32) | collective-permute-done | bytes 327712 | tf_op jit(solution)/shard_map/ppermute | solution.py:28
  61.1 2.4 broadcast_select_fusion.13
  68.3 1.6 copy-done.16
  70.4 2.3 fusion.25
  72.8 4.1 %collective-permute-start.4 = (bf16[512,512]{1,0:T(8,128)(2,1)}, bf16[512,512]{1,0:T(8,128)(2,1)}, u32[]{:S(2)}, u32[]{:S(2)}) collective-permute-start(bf16[512,512]{1,0:T(8,128)(2,1)} %fusion.25), channel_id=1, source_target_pairs={{0,4},{4,8},{8,12},{12,16},{16,20},{20,24},{24,28},{1,5},{5,9},{9,... | collective-permute-start | bytes 1572872 | tf_op jit(solution)/shard_map/ppermute | solution.py:33
  76.9 3.5 %collective-permute-start.3 = (bf16[512,512]{1,0:T(8,128)(2,1)}, bf16[512,512]{1,0:T(8,128)(2,1)}, u32[]{:S(2)}, u32[]{:S(2)}) collective-permute-start(bf16[512,512]{1,0:T(8,128)(2,1)} %fusion.25), channel_id=1, source_target_pairs={{0,8},{4,12},{8,16},{12,20},{16,24},{20,28},{1,9},{5,13},{9,17},{1... | collective-permute-start | bytes 1572872 | tf_op jit(solution)/shard_map/ppermute | solution.py:33
  80.4 1.6 pad_maximum_fusion.1
  82.0 4.4 %copy.15 = bf16[512,2560]{0,1:T(8,128)(2,1)} copy(bf16[512,2560]{1,0:T(8,128)(2,1)} %pad_maximum_fusion.1) | data formatting | bytes 5242880 | tf_op jit(solution)/shard_map/concatenate | solution.py:45
  86.4 3.0 %slice_select_fusion.1 = bf16[512,4,1,320]{0,3,2,1:T(8,128)(2,1)} fusion(bf16[512,4,2,320]{0,3,2,1:T(8,128)(2,1)} %bitcast.86, pred[]{:T(512)S(6)} %eq.15), kind=kLoop, calls=%fused_computation.48 | loop fusion | flops 655360 | bytes 3932161 | tf_op jit(solution)/shard_map/jit(_where)/select_n | solution.py:105
  91.0 2.4 convolution_convert_fusion.4
  95.6 1.6 pad_maximum_fusion.2
  97.2 4.4 %copy.17 = bf16[512,2560]{0,1:T(8,128)(2,1)} copy(bf16[512,2560]{1,0:T(8,128)(2,1)} %pad_maximum_fusion.2) | data formatting | bytes 5242880 | tf_op jit(solution)/shard_map/concatenate | solution.py:45
  101.6 2.0 slice_select_fusion
  103.9 3.3 %convolution_convert_fusion.3 = bf16[512,512]{0,1:T(8,128)(2,1)S(1)} fusion(bf16[512,2560]{1,0:T(8,128)(2,1)} %param.11, bf16[512,640]{1,0:T(8,128)(2,1)S(1)} %copy-done.13, bf16[512,640]{1,0:T(8,128)(2,1)S(1)} %get-tuple-element.27, bf16[512,640]{1,0:T(8,128)(2,1)S(1)} %copy-done.11, bf16[512,640]{1,0:T(8,128)(2,1)S(1)} %copy-done.9), kind=kOutput, calls=%fused_computation.54 | convolution fusion | flops 1352925184 | bytes 5767168 | tf_op jit(solution)/shard_map/dot_general | solution.py:23
  107.2 1.5 pad_maximum_fusion.3
  121.4 1.6 collective-permute-start.35
  126.6 1.6 fusion.88
  128.2 18.4 %collective-permute-done.35 = bf16[512,512]{0,1:T(8,128)(2,1)S(1)} collective-permute-done((bf16[512,512]{0,1:T(8,128)(2,1)S(1)}, bf16[512,512]{0,1:T(8,128)(2,1)S(1)}, u32[]{:S(2)}, u32[]{:S(2)}) %collective-permute-start.35) | collective-permute-done | bytes 524320 | tf_op jit(solution)/shard_map/ppermute | solution.py:28
  146.6 1.6 convolution_convert_fusion
  148.2 2.9 %collective-permute-start.36 = (bf16[320,512]{1,0:T(8,128)(2,1)S(1)}, bf16[320,512]{1,0:T(8,128)(2,1)S(1)}, u32[]{:S(2)}, u32[]{:S(2)}) collective-permute-start(bf16[320,512]{1,0:T(8,128)(2,1)S(1)} %get-tuple-element.13), channel_id=1, source_target_pairs={{0,8},{4,12},{1,9},{5,13},{2,10},{6,14},{3,11},{7,15}} | collective-permute-start | bytes 983048 | tf_op jit(solution)/shard_map/ppermute | solution.py:80
  151.8 5.5 %collective-permute-done.8 = bf16[512,512]{0,1:T(8,128)(2,1)S(1)} collective-permute-done((bf16[512,512]{0,1:T(8,128)(2,1)S(1)}, bf16[512,512]{0,1:T(8,128)(2,1)S(1)}, u32[]{:S(2)}, u32[]{:S(2)}) %collective-permute-start.8) | collective-permute-done | bytes 524320 | tf_op jit(solution)/shard_map/ppermute | solution.py:33
  159.2 1.6 convolution_convert_fusion.2
  160.8 2.7 %collective-permute-start.18 = (bf16[320,512]{1,0:T(8,128)(2,1)S(1)}, bf16[320,512]{1,0:T(8,128)(2,1)S(1)}, u32[]{:S(2)}, u32[]{:S(2)}) collective-permute-start(bf16[320,512]{1,0:T(8,128)(2,1)S(1)} %get-tuple-element.21), channel_id=1, source_target_pairs={{0,8},{4,12},{1,9},{5,13},{2,10},{6,14},{3,11},{7,15}} | collective-permute-start | bytes 983048 | tf_op jit(solution)/shard_map/ppermute | solution.py:80
  165.5 3.7 %collective-permute-done.18 = bf16[320,512]{1,0:T(8,128)(2,1)S(1)} collective-permute-done((bf16[320,512]{1,0:T(8,128)(2,1)S(1)}, bf16[320,512]{1,0:T(8,128)(2,1)S(1)}, u32[]{:S(2)}, u32[]{:S(2)}) %collective-permute-start.18) | collective-permute-done | bytes 327712 | tf_op jit(solution)/shard_map/ppermute | solution.py:80
  169.2 4.4 %collective-permute-start.37 = (bf16[320,512]{1,0:T(8,128)(2,1)S(1)}, bf16[320,512]{1,0:T(8,128)(2,1)S(1)}, u32[]{:S(2)}, u32[]{:S(2)}) collective-permute-start(bf16[320,512]{1,0:T(8,128)(2,1)S(1)} %fusion.47), channel_id=1, source_target_pairs={{0,8},{4,12},{8,16},{12,20},{1,9},{5,13},{9,17},{13,21},{2,10},{6,... | collective-permute-start | bytes 983048 | tf_op jit(solution)/shard_map/ppermute | solution.py:80
  173.8 1.9 collective-permute-start.19
  175.7 1.6 convolution_convert_fusion.1
  177.4 4.4 %collective-permute-done.37 = bf16[320,512]{1,0:T(8,128)(2,1)S(1)} collective-permute-done((bf16[320,512]{1,0:T(8,128)(2,1)S(1)}, bf16[320,512]{1,0:T(8,128)(2,1)S(1)}, u32[]{:S(2)}, u32[]{:S(2)}) %collective-permute-start.37) | collective-permute-done | bytes 327712 | tf_op jit(solution)/shard_map/ppermute | solution.py:80
  181.8 4.4 %collective-permute-start.25 = (bf16[320,512]{1,0:T(8,128)(2,1)S(1)}, bf16[320,512]{1,0:T(8,128)(2,1)S(1)}, u32[]{:S(2)}, u32[]{:S(2)}) collective-permute-start(bf16[320,512]{1,0:T(8,128)(2,1)S(1)} %get-tuple-element.17), channel_id=1, source_target_pairs={{0,8},{4,12},{1,9},{5,13},{2,10},{6,14},{3,11},{7,15}} | collective-permute-start | bytes 983048 | tf_op jit(solution)/shard_map/ppermute | solution.py:80
  187.1 1.7 collective-permute-done.19
  188.8 4.4 %collective-permute-start.38 = (bf16[320,512]{1,0:T(8,128)(2,1)S(1)}, bf16[320,512]{1,0:T(8,128)(2,1)S(1)}, u32[]{:S(2)}, u32[]{:S(2)}) collective-permute-start(bf16[320,512]{1,0:T(8,128)(2,1)S(1)} %get-tuple-element.11), channel_id=1, source_target_pairs={{0,8},{4,12},{8,16},{12,20},{16,24},{20,28},{1,9},{5,13},{9,17},{1... | collective-permute-start | bytes 983048 | tf_op jit(solution)/shard_map/ppermute | solution.py:80
  193.4 2.4 collective-permute-done.25
  196.6 5.0 %collective-permute-start.20 = (bf16[320,512]{1,0:T(8,128)(2,1)S(1)}, bf16[320,512]{1,0:T(8,128)(2,1)S(1)}, u32[]{:S(2)}, u32[]{:S(2)}) collective-permute-start(bf16[320,512]{1,0:T(8,128)(2,1)S(1)} %get-tuple-element.19), channel_id=1, source_target_pairs={{0,8},{4,12},{8,16},{12,20},{16,24},{20,28},{1,9},{5,13},{9,17},{1... | collective-permute-start | bytes 983048 | tf_op jit(solution)/shard_map/ppermute | solution.py:80
  201.6 4.6 %collective-permute-start.26 = (bf16[320,512]{1,0:T(8,128)(2,1)S(1)}, bf16[320,512]{1,0:T(8,128)(2,1)S(1)}, u32[]{:S(2)}, u32[]{:S(2)}) collective-permute-start(bf16[320,512]{1,0:T(8,128)(2,1)S(1)} %fusion.53), channel_id=1, source_target_pairs={{0,8},{4,12},{8,16},{12,20},{1,9},{5,13},{9,17},{13,21},{2,10},{6,... | collective-permute-start | bytes 983048 | tf_op jit(solution)/shard_map/ppermute | solution.py:80
  207.5 1.6 collective-permute-start.12
  209.1 4.4 %collective-permute-done.26 = bf16[320,512]{1,0:T(8,128)(2,1)S(1)} collective-permute-done((bf16[320,512]{1,0:T(8,128)(2,1)S(1)}, bf16[320,512]{1,0:T(8,128)(2,1)S(1)}, u32[]{:S(2)}, u32[]{:S(2)}) %collective-permute-start.26) | collective-permute-done | bytes 327712 | tf_op jit(solution)/shard_map/ppermute | solution.py:80
  217.1 9.0 %collective-permute-done.41 = bf16[320,512]{1,0:T(8,128)(2,1)S(1)} collective-permute-done((bf16[320,512]{1,0:T(8,128)(2,1)S(1)}, bf16[320,512]{1,0:T(8,128)(2,1)S(1)}, u32[]{:S(2)}, u32[]{:S(2)}) %collective-permute-start.41) | collective-permute-done | bytes 327712 | tf_op jit(solution)/shard_map/ppermute | solution.py:81
  226.1 4.4 %collective-permute-start.27 = (bf16[320,512]{1,0:T(8,128)(2,1)S(1)}, bf16[320,512]{1,0:T(8,128)(2,1)S(1)}, u32[]{:S(2)}, u32[]{:S(2)}) collective-permute-start(bf16[320,512]{1,0:T(8,128)(2,1)S(1)} %get-tuple-element.15), channel_id=1, source_target_pairs={{0,8},{4,12},{8,16},{12,20},{16,24},{20,28},{1,9},{5,13},{9,17},{1... | collective-permute-start | bytes 983048 | tf_op jit(solution)/shard_map/ppermute | solution.py:80
  233.8 1.5 add_convert_fusion.1
  235.3 7.3 %collective-permute-done.30 = bf16[320,512]{1,0:T(8,128)(2,1)S(1)} collective-permute-done((bf16[320,512]{1,0:T(8,128)(2,1)S(1)}, bf16[320,512]{1,0:T(8,128)(2,1)S(1)}, u32[]{:S(2)}, u32[]{:S(2)}) %collective-permute-start.30) | collective-permute-done | bytes 327712 | tf_op jit(solution)/shard_map/ppermute | solution.py:81
  (174 shorter events, 48.7 us)
Async XLA Ops:
  0.6 90.3 %copy-start = (bf16[2560,512]{1,0:T(8,128)(2,1)S(1)}, bf16[2560,512]{1,0:T(8,128)(2,1)}, u32[]{:S(2)}) copy-start(bf16[2560,512]{1,0:T(8,128)(2,1)} %param.8) | copy-start | bytes 7864324
  2.9 11.8 %collective-permute-start.13 = (bf16[512,320]{0,1:T(8,128)(2,1)}, bf16[512,320]{0,1:T(8,128)(2,1)}, u32[]{:S(2)}, u32[]{:S(2)}) collective-permute-start(bf16[512,320]{0,1:T(8,128)(2,1)} %fusion.70), channel_id=1, source_target_pairs={{0,4},{4,0},{8,12},{12,8},{16,20},{20,16},{24,28},{28,24},{1,5},{5... | collective-permute-start | bytes 983048 | tf_op jit(solution)/shard_map/ppermute | solution.py:28
  8.0 51.7 %copy-start.14 = (bf16[512,640]{1,0:T(8,128)(2,1)S(1)}, bf16[512,640]{1,0:T(8,128)(2,1)}, u32[]{:S(2)}) copy-start(bf16[512,640]{1,0:T(8,128)(2,1)} %param.7) | copy-start | bytes 1966084
  8.0 12.9 %collective-permute-start.31 = (bf16[512,320]{0,1:T(8,128)(2,1)}, bf16[512,320]{0,1:T(8,128)(2,1)}, u32[]{:S(2)}, u32[]{:S(2)}) collective-permute-start(bf16[512,320]{0,1:T(8,128)(2,1)} %fusion.69), channel_id=1, source_target_pairs={{0,4},{4,0},{8,12},{12,8},{16,20},{20,16},{24,28},{28,24},{1,5},{5... | collective-permute-start | bytes 983048 | tf_op jit(solution)/shard_map/ppermute | solution.py:28
  14.7 11.0 %collective-permute-start.14 = (bf16[512,320]{0,1:T(8,128)(2,1)}, bf16[512,320]{0,1:T(8,128)(2,1)}, u32[]{:S(2)}, u32[]{:S(2)}) collective-permute-start(bf16[512,320]{0,1:T(8,128)(2,1)} %collective-permute-done.13), channel_id=1, source_target_pairs={{0,2},{1,3},{2,0},{3,1},{4,6},{5,7},{6,4},{7,5},{8,10},{9,11},{10,... | collective-permute-start | bytes 983048 | tf_op jit(solution)/shard_map/ppermute | solution.py:28
  16.8 42.5 %collective-permute-start = (bf16[512,640]{1,0:T(8,128)(2,1)}, bf16[512,640]{1,0:T(8,128)(2,1)}, u32[]{:S(2)}, u32[]{:S(2)}) collective-permute-start(bf16[512,640]{1,0:T(8,128)(2,1)} %param.7), channel_id=1, source_target_pairs={{0,2},{1,3},{2,0},{3,1},{4,6},{5,7},{6,4},{7,5},{8,10},{9,11},{10,... | collective-permute-start | bytes 1966088 | tf_op jit(solution)/shard_map/ppermute | solution.py:28
  16.8 44.1 %collective-permute-start.5 = (bf16[512,640]{1,0:T(8,128)(2,1)}, bf16[512,640]{1,0:T(8,128)(2,1)}, u32[]{:S(2)}, u32[]{:S(2)}) collective-permute-start(bf16[512,640]{1,0:T(8,128)(2,1)} %param.12), channel_id=1, source_target_pairs={{0,2},{1,3},{2,0},{3,1},{4,6},{5,7},{6,4},{7,5},{8,10},{9,11},{10,... | collective-permute-start | bytes 1966088 | tf_op jit(solution)/shard_map/ppermute | solution.py:28
  20.9 37.2 %collective-permute-start.32 = (bf16[512,320]{0,1:T(8,128)(2,1)}, bf16[512,320]{0,1:T(8,128)(2,1)S(1)}, u32[]{:S(2)}, u32[]{:S(2)}) collective-permute-start(bf16[512,320]{0,1:T(8,128)(2,1)} %collective-permute-done.31), channel_id=1, source_target_pairs={{0,2},{1,3},{2,0},{3,1},{4,6},{5,7},{6,4},{7,5},{8,10},{9,11},{10,... | collective-permute-start | bytes 983048 | tf_op jit(solution)/shard_map/ppermute | solution.py:28
  22.6 38.5 %copy-start.15 = (bf16[512,640]{1,0:T(8,128)(2,1)S(1)}, bf16[512,640]{1,0:T(8,128)(2,1)}, u32[]{:S(2)}) copy-start(bf16[512,640]{1,0:T(8,128)(2,1)} %param.12) | copy-start | bytes 1966084
  26.8 36.6 %collective-permute-start.15 = (bf16[512,320]{0,1:T(8,128)(2,1)S(1)}, bf16[512,320]{0,1:T(8,128)(2,1)S(1)}, u32[]{:S(2)}, u32[]{:S(2)}) collective-permute-start(bf16[512,320]{0,1:T(8,128)(2,1)S(1)} %get-tuple-element.45), channel_id=1, source_target_pairs={{0,1},{1,0},{2,3},{3,2},{4,5},{5,4},{6,7},{7,6},{8,9},{9,8},{10,11... | collective-permute-start | bytes 983048 | tf_op jit(solution)/shard_map/ppermute | solution.py:28
  26.9 37.9 %collective-permute-start.16 = (bf16[512,320]{0,1:T(8,128)(2,1)S(1)}, bf16[512,320]{0,1:T(8,128)(2,1)S(1)}, u32[]{:S(2)}, u32[]{:S(2)}) collective-permute-start(bf16[512,320]{0,1:T(8,128)(2,1)S(1)} %get-tuple-element.46), channel_id=1, source_target_pairs={{0,1},{1,0},{2,3},{3,2},{4,5},{5,4},{6,7},{7,6},{8,9},{9,8},{10,11... | collective-permute-start | bytes 983048 | tf_op jit(solution)/shard_map/ppermute | solution.py:28
  59.1 6.6 %collective-permute-start.33 = (bf16[512,320]{0,1:T(8,128)(2,1)S(1)}, bf16[512,320]{0,1:T(8,128)(2,1)S(1)}, u32[]{:S(2)}, u32[]{:S(2)}) collective-permute-start(bf16[512,320]{0,1:T(8,128)(2,1)S(1)} %get-tuple-element.37), channel_id=1, source_target_pairs={{0,1},{1,0},{2,3},{3,2},{4,5},{5,4},{6,7},{7,6},{8,9},{9,8},{10,11... | collective-permute-start | bytes 983048 | tf_op jit(solution)/shard_map/ppermute | solution.py:28
  59.2 7.8 %collective-permute-start.34 = (bf16[512,320]{0,1:T(8,128)(2,1)S(1)}, bf16[512,320]{0,1:T(8,128)(2,1)S(1)}, u32[]{:S(2)}, u32[]{:S(2)}) collective-permute-start(bf16[512,320]{0,1:T(8,128)(2,1)S(1)} %get-tuple-element.38), channel_id=1, source_target_pairs={{0,1},{1,0},{2,3},{3,2},{4,5},{5,4},{6,7},{7,6},{8,9},{9,8},{10,11... | collective-permute-start | bytes 983048 | tf_op jit(solution)/shard_map/ppermute | solution.py:28
  61.0 7.1 %collective-permute-start.1 = (bf16[512,640]{1,0:T(8,128)(2,1)S(1)}, bf16[512,640]{1,0:T(8,128)(2,1)S(1)}, u32[]{:S(2)}, u32[]{:S(2)}) collective-permute-start(bf16[512,640]{1,0:T(8,128)(2,1)S(1)} %get-tuple-element.31), channel_id=1, source_target_pairs={{0,1},{1,0},{2,3},{3,2},{4,5},{5,4},{6,7},{7,6},{8,9},{9,8},{10,11... | collective-permute-start | bytes 1966088 | tf_op jit(solution)/shard_map/ppermute | solution.py:28
  63.5 4.7 %collective-permute-start.2 = (bf16[512,640]{1,0:T(8,128)(2,1)S(1)}, bf16[512,640]{1,0:T(8,128)(2,1)S(1)}, u32[]{:S(2)}, u32[]{:S(2)}) collective-permute-start(bf16[512,640]{1,0:T(8,128)(2,1)S(1)} %get-tuple-element.32), channel_id=1, source_target_pairs={{0,1},{1,0},{2,3},{3,2},{4,5},{5,4},{6,7},{7,6},{8,9},{9,8},{10,11... | collective-permute-start | bytes 1966088 | tf_op jit(solution)/shard_map/ppermute | solution.py:28
  64.8 24.7 %collective-permute-start.6 = (bf16[512,640]{1,0:T(8,128)(2,1)}, bf16[512,640]{1,0:T(8,128)(2,1)}, u32[]{:S(2)}, u32[]{:S(2)}) collective-permute-start(bf16[512,640]{1,0:T(8,128)(2,1)} %get-tuple-element.25), channel_id=1, source_target_pairs={{0,1},{1,0},{2,3},{3,2},{4,5},{5,4},{6,7},{7,6},{8,9},{9,8},{10,11... | collective-permute-start | bytes 1966088 | tf_op jit(solution)/shard_map/ppermute | solution.py:28
  65.8 27.6 %collective-permute-start.7 = (bf16[512,640]{1,0:T(8,128)(2,1)}, bf16[512,640]{1,0:T(8,128)(2,1)}, u32[]{:S(2)}, u32[]{:S(2)}) collective-permute-start(bf16[512,640]{1,0:T(8,128)(2,1)} %get-tuple-element.26), channel_id=1, source_target_pairs={{0,1},{1,0},{2,3},{3,2},{4,5},{5,4},{6,7},{7,6},{8,9},{9,8},{10,11... | collective-permute-start | bytes 1966088 | tf_op jit(solution)/shard_map/ppermute | solution.py:28
  72.8 34.4 %collective-permute-start.4 = (bf16[512,512]{1,0:T(8,128)(2,1)}, bf16[512,512]{1,0:T(8,128)(2,1)}, u32[]{:S(2)}, u32[]{:S(2)}) collective-permute-start(bf16[512,512]{1,0:T(8,128)(2,1)} %fusion.25), channel_id=1, source_target_pairs={{0,4},{4,8},{8,12},{12,16},{16,20},{20,24},{24,28},{1,5},{5,9},{9,... | collective-permute-start | bytes 1572872 | tf_op jit(solution)/shard_map/ppermute | solution.py:33
  76.9 30.3 %collective-permute-start.3 = (bf16[512,512]{1,0:T(8,128)(2,1)}, bf16[512,512]{1,0:T(8,128)(2,1)}, u32[]{:S(2)}, u32[]{:S(2)}) collective-permute-start(bf16[512,512]{1,0:T(8,128)(2,1)} %fusion.25), channel_id=1, source_target_pairs={{0,8},{4,12},{8,16},{12,20},{16,24},{20,28},{1,9},{5,13},{9,17},{1... | collective-permute-start | bytes 1572872 | tf_op jit(solution)/shard_map/ppermute | solution.py:33
  121.4 25.2 %collective-permute-start.35 = (bf16[512,512]{0,1:T(8,128)(2,1)S(1)}, bf16[512,512]{0,1:T(8,128)(2,1)S(1)}, u32[]{:S(2)}, u32[]{:S(2)}) collective-permute-start(bf16[512,512]{0,1:T(8,128)(2,1)S(1)} %pad_maximum_fusion.5), channel_id=1, source_target_pairs={{0,4},{4,0},{8,12},{12,8},{16,20},{20,16},{24,28},{28,24},{1,5},{5... | collective-permute-start | bytes 1572872 | tf_op jit(solution)/shard_map/ppermute | solution.py:28
  123.0 35.5 %collective-permute-start.17 = (bf16[512,512]{0,1:T(8,128)(2,1)S(1)}, bf16[512,512]{0,1:T(8,128)(2,1)S(1)}, u32[]{:S(2)}, u32[]{:S(2)}) collective-permute-start(bf16[512,512]{0,1:T(8,128)(2,1)S(1)} %pad_maximum_fusion.4), channel_id=1, source_target_pairs={{0,4},{4,0},{8,12},{12,8},{16,20},{20,16},{24,28},{28,24},{1,5},{5... | collective-permute-start | bytes 1572872 | tf_op jit(solution)/shard_map/ppermute | solution.py:28
  123.8 33.4 %collective-permute-start.8 = (bf16[512,512]{0,1:T(8,128)(2,1)S(1)}, bf16[512,512]{0,1:T(8,128)(2,1)S(1)}, u32[]{:S(2)}, u32[]{:S(2)}) collective-permute-start(bf16[512,512]{0,1:T(8,128)(2,1)S(1)} %get-tuple-element.9), channel_id=1, source_target_pairs={{4,0},{8,4},{12,8},{16,12},{20,16},{24,20},{28,24},{5,1},{9,5},{13... | collective-permute-start | bytes 1572872 | tf_op jit(solution)/shard_map/ppermute | solution.py:33
  125.1 21.4 %copy-start.26 = (bf16[512,320]{0,1:T(8,128)(2,1)S(1)}, bf16[512,320]{0,1:T(8,128)(2,1)}, u32[]{:S(2)}) copy-start(bf16[512,320]{0,1:T(8,128)(2,1)} %get-tuple-element.35) | copy-start | bytes 983044
  125.1 21.4 %copy-start.27 = (bf16[512,320]{0,1:T(8,128)(2,1)S(1)}, bf16[512,320]{0,1:T(8,128)(2,1)}, u32[]{:S(2)}) copy-start(bf16[512,320]{0,1:T(8,128)(2,1)} %get-tuple-element.36) | copy-start | bytes 983044
  125.2 21.4 %copy-start.28 = (bf16[512,320]{0,1:T(8,128)(2,1)S(1)}, bf16[512,320]{0,1:T(8,128)(2,1)}, u32[]{:S(2)}) copy-start(bf16[512,320]{0,1:T(8,128)(2,1)} %get-tuple-element.39) | copy-start | bytes 983044
  125.2 32.1 %collective-permute-start.9 = (bf16[512,512]{0,1:T(8,128)(2,1)S(1)}, bf16[512,512]{0,1:T(8,128)(2,1)S(1)}, u32[]{:S(2)}, u32[]{:S(2)}) collective-permute-start(bf16[512,512]{0,1:T(8,128)(2,1)S(1)} %get-tuple-element.10), channel_id=1, source_target_pairs={{8,0},{12,4},{16,8},{20,12},{24,16},{28,20},{9,1},{13,5},{17,9},{2... | collective-permute-start | bytes 1572872 | tf_op jit(solution)/shard_map/ppermute | solution.py:33
  148.2 17.1 %collective-permute-start.36 = (bf16[320,512]{1,0:T(8,128)(2,1)S(1)}, bf16[320,512]{1,0:T(8,128)(2,1)S(1)}, u32[]{:S(2)}, u32[]{:S(2)}) collective-permute-start(bf16[320,512]{1,0:T(8,128)(2,1)S(1)} %get-tuple-element.13), channel_id=1, source_target_pairs={{0,8},{4,12},{1,9},{5,13},{2,10},{6,14},{3,11},{7,15}} | collective-permute-start | bytes 983048 | tf_op jit(solution)/shard_map/ppermute | solution.py:80
  151.1 26.2 %collective-permute-start.39 = (bf16[320,512]{1,0:T(8,128)(2,1)S(1)}, bf16[320,512]{1,0:T(8,128)(2,1)S(1)}, u32[]{:S(2)}, u32[]{:S(2)}) collective-permute-start(bf16[320,512]{1,0:T(8,128)(2,1)S(1)} %get-tuple-element.14), channel_id=1, source_target_pairs={{24,16},{28,20},{25,17},{29,21},{26,18},{30,22},{27,19},{31,23}} | collective-permute-start | bytes 983048 | tf_op jit(solution)/shard_map/ppermute | solution.py:81
  157.6 16.2 %collective-permute-start.24 = (bf16[512,512]{0,1:T(8,128)(2,1)S(1)}, bf16[512,512]{0,1:T(8,128)(2,1)S(1)}, u32[]{:S(2)}, u32[]{:S(2)}) collective-permute-start(bf16[512,512]{0,1:T(8,128)(2,1)S(1)} %fusion.31), channel_id=1, source_target_pairs={{0,4},{4,0},{8,12},{12,8},{16,20},{20,16},{24,28},{28,24},{1,5},{5... | collective-permute-start | bytes 1572872 | tf_op jit(solution)/shard_map/ppermute | solution.py:28
  160.8 8.5 %collective-permute-start.18 = (bf16[320,512]{1,0:T(8,128)(2,1)S(1)}, bf16[320,512]{1,0:T(8,128)(2,1)S(1)}, u32[]{:S(2)}, u32[]{:S(2)}) collective-permute-start(bf16[320,512]{1,0:T(8,128)(2,1)S(1)} %get-tuple-element.21), channel_id=1, source_target_pairs={{0,8},{4,12},{1,9},{5,13},{2,10},{6,14},{3,11},{7,15}} | collective-permute-start | bytes 983048 | tf_op jit(solution)/shard_map/ppermute | solution.py:80
  163.5 22.8 %collective-permute-start.21 = (bf16[320,512]{1,0:T(8,128)(2,1)S(1)}, bf16[320,512]{1,0:T(8,128)(2,1)S(1)}, u32[]{:S(2)}, u32[]{:S(2)}) collective-permute-start(bf16[320,512]{1,0:T(8,128)(2,1)S(1)} %get-tuple-element.22), channel_id=1, source_target_pairs={{24,16},{28,20},{25,17},{29,21},{26,18},{30,22},{27,19},{31,23}} | collective-permute-start | bytes 983048 | tf_op jit(solution)/shard_map/ppermute | solution.py:81
  165.3 31.3 %collective-permute-start.11 = (bf16[512,640]{1,0:T(8,128)(2,1)S(1)}, bf16[512,640]{1,0:T(8,128)(2,1)S(1)}, u32[]{:S(2)}, u32[]{:S(2)}) collective-permute-start(bf16[512,640]{1,0:T(8,128)(2,1)S(1)} %get-tuple-element.7), channel_id=1, source_target_pairs={{0,1},{1,0},{2,3},{3,2},{4,5},{5,4},{6,7},{7,6},{8,9},{9,8},{10,11... | collective-permute-start | bytes 1966088 | tf_op jit(solution)/shard_map/ppermute | solution.py:28
  169.2 12.5 %collective-permute-start.37 = (bf16[320,512]{1,0:T(8,128)(2,1)S(1)}, bf16[320,512]{1,0:T(8,128)(2,1)S(1)}, u32[]{:S(2)}, u32[]{:S(2)}) collective-permute-start(bf16[320,512]{1,0:T(8,128)(2,1)S(1)} %fusion.47), channel_id=1, source_target_pairs={{0,8},{4,12},{8,16},{12,20},{1,9},{5,13},{9,17},{13,21},{2,10},{6,... | collective-permute-start | bytes 983048 | tf_op jit(solution)/shard_map/ppermute | solution.py:80
  173.8 15.0 %collective-permute-start.19 = (bf16[320,512]{1,0:T(8,128)(2,1)S(1)}, bf16[320,512]{1,0:T(8,128)(2,1)S(1)}, u32[]{:S(2)}, u32[]{:S(2)}) collective-permute-start(bf16[320,512]{1,0:T(8,128)(2,1)S(1)} %fusion.58), channel_id=1, source_target_pairs={{0,8},{4,12},{8,16},{12,20},{1,9},{5,13},{9,17},{13,21},{2,10},{6,... | collective-permute-start | bytes 983048 | tf_op jit(solution)/shard_map/ppermute | solution.py:80
  177.3 24.3 %collective-permute-start.10 = (bf16[512,640]{1,0:T(8,128)(2,1)S(1)}, bf16[512,640]{1,0:T(8,128)(2,1)S(1)}, u32[]{:S(2)}, u32[]{:S(2)}) collective-permute-start(bf16[512,640]{1,0:T(8,128)(2,1)S(1)} %get-tuple-element.8), channel_id=1, source_target_pairs={{0,1},{1,0},{2,3},{3,2},{4,5},{5,4},{6,7},{7,6},{8,9},{9,8},{10,11... | collective-permute-start | bytes 1966088 | tf_op jit(solution)/shard_map/ppermute | solution.py:28
  181.8 14.0 %collective-permute-start.25 = (bf16[320,512]{1,0:T(8,128)(2,1)S(1)}, bf16[320,512]{1,0:T(8,128)(2,1)S(1)}, u32[]{:S(2)}, u32[]{:S(2)}) collective-permute-start(bf16[320,512]{1,0:T(8,128)(2,1)S(1)} %get-tuple-element.17), channel_id=1, source_target_pairs={{0,8},{4,12},{1,9},{5,13},{2,10},{6,14},{3,11},{7,15}} | collective-permute-start | bytes 983048 | tf_op jit(solution)/shard_map/ppermute | solution.py:80
  186.4 21.2 %collective-permute-start.28 = (bf16[320,512]{1,0:T(8,128)(2,1)S(1)}, bf16[320,512]{1,0:T(8,128)(2,1)S(1)}, u32[]{:S(2)}, u32[]{:S(2)}) collective-permute-start(bf16[320,512]{1,0:T(8,128)(2,1)S(1)} %get-tuple-element.18), channel_id=1, source_target_pairs={{24,16},{28,20},{25,17},{29,21},{26,18},{30,22},{27,19},{31,23}} | collective-permute-start | bytes 983048 | tf_op jit(solution)/shard_map/ppermute | solution.py:81
  188.8 27.0 %collective-permute-start.38 = (bf16[320,512]{1,0:T(8,128)(2,1)S(1)}, bf16[320,512]{1,0:T(8,128)(2,1)S(1)}, u32[]{:S(2)}, u32[]{:S(2)}) collective-permute-start(bf16[320,512]{1,0:T(8,128)(2,1)S(1)} %get-tuple-element.11), channel_id=1, source_target_pairs={{0,8},{4,12},{8,16},{12,20},{16,24},{20,28},{1,9},{5,13},{9,17},{1... | collective-permute-start | bytes 983048 | tf_op jit(solution)/shard_map/ppermute | solution.py:80
  195.8 10.9 %collective-permute-start.40 = (bf16[320,512]{1,0:T(8,128)(2,1)S(1)}, bf16[320,512]{1,0:T(8,128)(2,1)S(1)}, u32[]{:S(2)}, u32[]{:S(2)}) collective-permute-start(bf16[320,512]{1,0:T(8,128)(2,1)S(1)} %get-tuple-element.12), channel_id=1, source_target_pairs={{16,8},{20,12},{24,16},{28,20},{17,9},{21,13},{25,17},{29,21},{18,... | collective-permute-start | bytes 983048 | tf_op jit(solution)/shard_map/ppermute | solution.py:81
  196.6 36.2 %collective-permute-start.20 = (bf16[320,512]{1,0:T(8,128)(2,1)S(1)}, bf16[320,512]{1,0:T(8,128)(2,1)S(1)}, u32[]{:S(2)}, u32[]{:S(2)}) collective-permute-start(bf16[320,512]{1,0:T(8,128)(2,1)S(1)} %get-tuple-element.19), channel_id=1, source_target_pairs={{0,8},{4,12},{8,16},{12,20},{16,24},{20,28},{1,9},{5,13},{9,17},{1... | collective-permute-start | bytes 983048 | tf_op jit(solution)/shard_map/ppermute | solution.py:80
  201.6 11.9 %collective-permute-start.26 = (bf16[320,512]{1,0:T(8,128)(2,1)S(1)}, bf16[320,512]{1,0:T(8,128)(2,1)S(1)}, u32[]{:S(2)}, u32[]{:S(2)}) collective-permute-start(bf16[320,512]{1,0:T(8,128)(2,1)S(1)} %fusion.53), channel_id=1, source_target_pairs={{0,8},{4,12},{8,16},{12,20},{1,9},{5,13},{9,17},{13,21},{2,10},{6,... | collective-permute-start | bytes 983048 | tf_op jit(solution)/shard_map/ppermute | solution.py:80
  206.7 8.3 %collective-permute-start.22 = (bf16[320,512]{1,0:T(8,128)(2,1)S(1)}, bf16[320,512]{1,0:T(8,128)(2,1)S(1)}, u32[]{:S(2)}, u32[]{:S(2)}) collective-permute-start(bf16[320,512]{1,0:T(8,128)(2,1)S(1)} %get-tuple-element.20), channel_id=1, source_target_pairs={{16,8},{20,12},{24,16},{28,20},{17,9},{21,13},{25,17},{29,21},{18,... | collective-permute-start | bytes 983048 | tf_op jit(solution)/shard_map/ppermute | solution.py:81
  207.5 26.3 %collective-permute-start.12 = (bf16[512,640]{1,0:T(8,128)(2,1)S(1)}, bf16[512,640]{1,0:T(8,128)(2,1)S(1)}, u32[]{:S(2)}, u32[]{:S(2)}) collective-permute-start(bf16[512,640]{1,0:T(8,128)(2,1)S(1)} %select_convert_fusion), channel_id=1, source_target_pairs={{0,2},{1,3},{2,0},{3,1},{4,6},{5,7},{6,4},{7,5},{8,10},{9,11},{10,... | collective-permute-start | bytes 1966088 | tf_op jit(solution)/shard_map/ppermute | solution.py:28
  213.5 12.6 %collective-permute-start.41 = (bf16[320,512]{1,0:T(8,128)(2,1)S(1)}, bf16[320,512]{1,0:T(8,128)(2,1)S(1)}, u32[]{:S(2)}, u32[]{:S(2)}) collective-permute-start(bf16[320,512]{1,0:T(8,128)(2,1)S(1)} %fusion.46), channel_id=1, source_target_pairs={{8,0},{12,4},{16,8},{20,12},{24,16},{28,20},{9,1},{13,5},{17,9},{2... | collective-permute-start | bytes 983048 | tf_op jit(solution)/shard_map/ppermute | solution.py:81
  215.0 16.4 %collective-permute-start.29 = (bf16[320,512]{1,0:T(8,128)(2,1)S(1)}, bf16[320,512]{1,0:T(8,128)(2,1)S(1)}, u32[]{:S(2)}, u32[]{:S(2)}) collective-permute-start(bf16[320,512]{1,0:T(8,128)(2,1)S(1)} %get-tuple-element.16), channel_id=1, source_target_pairs={{16,8},{20,12},{24,16},{28,20},{17,9},{21,13},{25,17},{29,21},{18,... | collective-permute-start | bytes 983048 | tf_op jit(solution)/shard_map/ppermute | solution.py:81
  215.8 17.0 %collective-permute-start.23 = (bf16[320,512]{1,0:T(8,128)(2,1)S(1)}, bf16[320,512]{1,0:T(8,128)(2,1)S(1)}, u32[]{:S(2)}, u32[]{:S(2)}) collective-permute-start(bf16[320,512]{1,0:T(8,128)(2,1)S(1)} %fusion.57), channel_id=1, source_target_pairs={{8,0},{12,4},{16,8},{20,12},{24,16},{28,20},{9,1},{13,5},{17,9},{2... | collective-permute-start | bytes 983048 | tf_op jit(solution)/shard_map/ppermute | solution.py:81
  226.1 9.2 %collective-permute-start.27 = (bf16[320,512]{1,0:T(8,128)(2,1)S(1)}, bf16[320,512]{1,0:T(8,128)(2,1)S(1)}, u32[]{:S(2)}, u32[]{:S(2)}) collective-permute-start(bf16[320,512]{1,0:T(8,128)(2,1)S(1)} %get-tuple-element.15), channel_id=1, source_target_pairs={{0,8},{4,12},{8,16},{12,20},{16,24},{20,28},{1,9},{5,13},{9,17},{1... | collective-permute-start | bytes 983048 | tf_op jit(solution)/shard_map/ppermute | solution.py:80
  231.5 11.1 %collective-permute-start.30 = (bf16[320,512]{1,0:T(8,128)(2,1)S(1)}, bf16[320,512]{1,0:T(8,128)(2,1)S(1)}, u32[]{:S(2)}, u32[]{:S(2)}) collective-permute-start(bf16[320,512]{1,0:T(8,128)(2,1)S(1)} %fusion.52), channel_id=1, source_target_pairs={{8,0},{12,4},{16,8},{20,12},{24,16},{28,20},{9,1},{13,5},{17,9},{2... | collective-permute-start | bytes 983048 | tf_op jit(solution)/shard_map/ppermute | solution.py:81
  (25 other events, 125.2 us)

commit v2 on v1

--- a/solution.py
+++ b/solution.py
@@ -1,8 +1,11 @@
+import functools
 import math
 
 import jax
 import jax.numpy as jnp
 from jax import lax
+from jax.experimental import pallas as pl
+from jax.experimental.pallas import tpu as pltpu
 from jax.sharding import PartitionSpec as P
 
 HEAD_SIZE = 256
@@ -53,36 +56,259 @@
     )
 
 
-def chain_sum(parts):
-    levels = parts.shape[0]
-    level = lax.axis_index("seq") // 2
-    up = down = None
-
-    def block(index):
-        return lax.dynamic_index_in_dim(parts, jnp.clip(index, 0, levels - 1), 0, keepdims=False)
-
-    def added(value, arrived):
-        if arrived is None:
-            return value
-        return (value.astype(F32) + arrived.astype(F32)).astype(BF16)
-
+def remote(source, target, send, recv, axis, index):
+    return pltpu.make_async_remote_copy(
+        src_ref=source,
+        dst_ref=target,
+        send_sem=send,
+        recv_sem=recv,
+        device_id={axis: index},
+        device_id_type=pl.DeviceIdType.MESH,
+    )
+
+
+def greet(barrier, peers):
+    for axis, index, here in peers:
+
+        @pl.when(here)
+        def _():
+            pl.semaphore_signal(
+                barrier, inc=1, device_id={axis: index}, device_id_type=pl.DeviceIdType.MESH
+            )
+
+    pl.semaphore_wait(barrier, sum(jnp.where(here, 1, 0) for _, _, here in peers))
+
+
+def exchange_kernel(
+    count, reach, pair, kv_own, halo, pair_near, kv_grad, kv_near,
+    landed, total, swap_send, swap_recv, halo_send, halo_recv,
+):
+    me = lax.axis_index("seq")
+    near = me + 1 - 2 * lax.rem(me, 2)
+    peers = []
+    for offset in range(1, reach + 1):
+        peers.append(("seq", me - offset, me >= offset))
+        peers.append(("seq", me + offset, me + offset < count))
+    greet(pltpu.get_barrier_semaphore(), peers)
+
+    def back(offset):
+        return remote(
+            halo.at[offset - 1], landed.at[offset - 1],
+            halo_send.at[offset - 1], halo_recv.at[offset - 1], "seq", me - offset,
+        )
+
+    for offset in range(reach, 0, -1):
+
+        @pl.when(me >= offset)
+        def _():
+            back(offset).start()
+
+    pair_copy = remote(pair, pair_near, swap_send.at[0], swap_recv.at[0], "seq", near)
+    pair_copy.start()
+    total[...] = kv_own[...]
+    for offset in range(reach, 0, -1):
+
+        @pl.when(me + offset < count)
+        def _():
+            back(offset).wait_recv()
+            total[...] += landed[offset - 1].astype(F32)
+
+    kv_grad[...] = total[...].astype(BF16)
+    kv_copy = remote(kv_grad, kv_near, swap_send.at[1], swap_recv.at[1], "seq", near)
+    kv_copy.start()
+    pair_copy.wait()
+    kv_copy.wait()
+    for offset in range(1, reach + 1):
+
+        @pl.when(me >= offset)
+        def _():
+            back(offset).wait_send()
+
+
+def exchange(pair, kv_own, halo):
+    count = lax.axis_size("seq")
+    reach = halo.shape[0]
+    vmem = pl.BlockSpec(memory_space=pltpu.VMEM)
+    return pl.pallas_call(
+        functools.partial(exchange_kernel, count, reach),
+        out_shape=[
+            jax.ShapeDtypeStruct(pair.shape, BF16),
+            jax.ShapeDtypeStruct(kv_own.shape, BF16),
+            jax.ShapeDtypeStruct(kv_own.shape, BF16),
+        ],
+        in_specs=[vmem] * 3,
+        out_specs=[vmem] * 3,
+        scratch_shapes=[
+            pltpu.VMEM(halo.shape, BF16),
+            pltpu.VMEM(kv_own.shape, F32),
+            pltpu.SemaphoreType.DMA((2,)),
+            pltpu.SemaphoreType.DMA((2,)),
+            pltpu.SemaphoreType.DMA((reach,)),
+            pltpu.SemaphoreType.DMA((reach,)),
+        ],
+        compiler_params=pltpu.CompilerParams(
+            collective_id=1, has_side_effects=True, vmem_limit_bytes=40 * 2**20
+        ),
+    )(pair, kv_own, halo)
+
+
+def sum_kernel(
+    levels, parts_a, parts_b, parts_c, term, out_a, out_b, out_c, hidden,
+    up_tx, up_rx, down_tx, down_rx, near_rx, far_tx, far_rx,
+    up_send, up_recv, down_send, down_recv, hid_send, hid_recv,
+):
+    parts = (parts_a, parts_b, parts_c)
+    outs = (out_a, out_b, out_c)
+    me = lax.axis_index("seq")
+    z = me // 2
+    tp = lax.axis_index("tp")
+    high, low = tp // 2, lax.rem(tp, 2)
+    near, far = tp + 1 - 2 * low, tp + 2 - 4 * high
+    width = hidden.shape[1]
+    always = tp >= 0
+    greet(
+        pltpu.get_barrier_semaphore(),
+        [
+            ("seq", me - 2, z >= 1),
+            ("seq", me + 2, z <= levels - 2),
+            ("tp", near, always),
+            ("tp", far, always),
+        ],
+    )
+
+    def columns(index):
+        return pl.ds(pl.multiple_of(index * width, width), width)
+
+    def near_copy(slot):
+        half = 1 - high if slot == 0 else high
+        return remote(
+            term.at[:, columns(2 * half + 1 - low)], near_rx.at[slot],
+            hid_send.at[slot], hid_recv.at[slot], "tp", near,
+        )
+
+    far_copy = remote(far_tx, far_rx, hid_send.at[2], hid_recv.at[2], "tp", far)
+
+    def up(step, c):
+        return remote(
+            up_tx.at[step, c], up_rx.at[step, c],
+            up_send.at[step, c], up_recv.at[step, c], "seq", me + 2,
+        )
+
+    def down(step, c):
+        return remote(
+            down_tx.at[step, c], down_rx.at[step, c],
+            down_send.at[step, c], down_recv.at[step, c], "seq", me - 2,
+        )
+
+    near_copy(0).start()
+    near_copy(1).start()
     for step in range(levels - 1):
         gap = levels - 1 - step
-        up_value = added(block(level + gap), up)
-        down_value = added(block(level - gap), down)
-        ups, downs = [], []
-        for z in range(levels):
-            for y in range(2):
-                if z <= step:
-                    ups.append((2 * z + y, 2 * z + 2 + y))
-                if z >= gap:
-                    downs.append((2 * z + y, 2 * z - 2 + y))
-        up = lax.ppermute(up_value, "seq", ups)
-        down = lax.ppermute(down_value, "seq", downs)
-    total = block(level).astype(F32)
-    if up is not None:
-        total = total + up.astype(F32) + down.astype(F32)
-    return total
+        for c in range(3):
+
+            @pl.when(z <= step)
+            def _():
+                @pl.when(z == 0)
+                def _():
+                    up_tx[step, c] = parts[c][z + gap]
+
+                if step > 0:
+
+                    @pl.when(z >= 1)
+                    def _():
+                        up(step - 1, c).wait_recv()
+                        up_tx[step, c] = (
+                            parts[c][z + gap].astype(F32) + up_rx[step - 1, c].astype(F32)
+                        ).astype(BF16)
+
+                up(step, c).start()
+
+            @pl.when(z >= gap)
+            def _():
+                @pl.when(z == levels - 1)
+                def _():
+                    down_tx[step, c] = parts[c][z - gap]
+
+                if step > 0:
+
+                    @pl.when(z <= levels - 2)
+                    def _():
+                        down(step - 1, c).wait_recv()
+                        down_tx[step, c] = (
+                            parts[c][z - gap].astype(F32) + down_rx[step - 1, c].astype(F32)
+                        ).astype(BF16)
+
+                down(step, c).start()
+
+        if step == 0:
+            near_copy(0).wait_recv()
+            far_tx[...] = (
+                term[:, columns(2 * (1 - high) + low)].astype(F32) + near_rx[0].astype(F32)
+            ).astype(BF16)
+            far_copy.start()
+    near_copy(1).wait_recv()
+    far_copy.wait_recv()
+    hidden[...] = (
+        term[:, columns(2 * high + low)].astype(F32)
+        + near_rx[1].astype(F32)
+        + far_rx[...].astype(F32)
+    ).astype(BF16)
+    last = levels - 2
+    for c in range(3):
+        outs[c][...] = parts[c][z].astype(F32)
+
+        @pl.when(z >= 1)
+        def _():
+            up(last, c).wait_recv()
+            outs[c][...] += up_rx[last, c].astype(F32)
+
+        @pl.when(z <= levels - 2)
+        def _():
+            down(last, c).wait_recv()
+            outs[c][...] += down_rx[last, c].astype(F32)
+
+    near_copy(0).wait_send()
+    near_copy(1).wait_send()
+    far_copy.wait_send()
+    for step in range(levels - 1):
+        for c in range(3):
+
+            @pl.when(z <= step)
+            def _():
+                up(step, c).wait_send()
+
+            @pl.when(z >= levels - 1 - step)
+            def _():
+                down(step, c).wait_send()
+
+
+def final_sums(parts_a, parts_b, parts_c, term):
+    levels, rows, columns = parts_a.shape
+    shard = term.shape[1] // lax.axis_size("tp")
+    vmem = pl.BlockSpec(memory_space=pltpu.VMEM)
+    steps = levels - 1
+    slots = pltpu.VMEM((steps, 3, rows, columns), BF16)
+    block = (term.shape[0], shard)
+    sems = pltpu.SemaphoreType.DMA((steps, 3))
+    return pl.pallas_call(
+        functools.partial(sum_kernel, levels),
+        out_shape=[jax.ShapeDtypeStruct((rows, columns), F32)] * 3
+        + [jax.ShapeDtypeStruct(block, BF16)],
+        in_specs=[vmem] * 4,
+        out_specs=[vmem] * 4,
+        scratch_shapes=[
+            slots, slots, slots, slots,
+            pltpu.VMEM((2,) + block, BF16),
+            pltpu.VMEM(block, BF16),
+            pltpu.VMEM(block, BF16),
+            sems, sems, sems, sems,
+            pltpu.SemaphoreType.DMA((3,)),
+            pltpu.SemaphoreType.DMA((3,)),
+        ],
+        compiler_params=pltpu.CompilerParams(
+            collective_id=2, has_side_effects=True, vmem_limit_bytes=50 * 2**20
+        ),
+    )(parts_a, parts_b, parts_c, term)
 
 
 def per_device(
@@ -98,13 +324,11 @@
     width = shard_width * tp_count
     piece = width // seq_count
 
-    def halves(array):
+    def theirs(array):
         split = array.reshape(tok_rows, -1, 2, piece)
         even = split[:, :, 0].reshape(tok_rows, -1)
         odd = split[:, :, 1].reshape(tok_rows, -1)
-        mine = jnp.where(parity == 0, even, odd)
-        theirs = jnp.where(parity == 0, odd, even)
-        return mine, theirs
+        return jnp.where(parity == 0, odd, even)
 
     full_hidden = gather_features(hidden_in)
     key_values = dot(full_hidden, jnp.concatenate([key_projection, value_projection], 1)).astype(BF16)
@@ -113,12 +337,13 @@
     query_matrix = dot(full_hidden, query_proj).astype(BF16)
     attention_gradient = right_transposed_dot(full_cotangent, output_proj).astype(BF16)
 
-    hidden_theirs = swap(halves(hidden_in)[1], "seq", 1)
-    cot_theirs = swap(halves(out_cotangent)[1], "seq", 1)
-    hidden_pair = jnp.concatenate(
-        [halves(full_hidden)[0], gather_features(hidden_theirs)], 0
-    )
-    cot_pair = jnp.concatenate([halves(full_cotangent)[0], gather_features(cot_theirs)], 0)
+    hidden_near = swap(theirs(hidden_in), "seq", 1)
+    cot_near = swap(theirs(out_cotangent), "seq", 1)
+    hidden_near, cot_near, query_matrix, attention_gradient = lax.optimization_barrier(
+        (hidden_near, cot_near, query_matrix, attention_gradient)
+    )
+    hidden_near = gather_features(hidden_near)
+    cot_near = gather_features(cot_near)
 
     kv_width = key_projection.shape[1]
     kv_heads = kv_width // HEAD_SIZE
@@ -159,48 +384,39 @@
     attention = jnp.concatenate(attention, 1)
     query_grad = jnp.concatenate(query_grad, 1)
     parts = jnp.concatenate(key_parts + value_parts, 1)
-    kv_total = parts[reach * tok_rows :]
-    for offset in range(1, reach + 1):
-        start = (reach - offset) * tok_rows
-        kv_total = kv_total + shift(
-            parts[start : start + tok_rows].astype(BF16), -offset
-        ).astype(F32)
-    kv_grad = kv_total.astype(BF16)
-
-    attention_pair = jnp.concatenate([attention, swap(attention, "seq", 1)], 0)
-    query_pair = jnp.concatenate([query_grad, swap(query_grad, "seq", 1)], 0)
-    kv_pair = jnp.concatenate([kv_grad, swap(kv_grad, "seq", 1)], 0)
-
-    def summed(left, right):
-        return chain_sum(
-            transposed_dot(left, right).astype(BF16).reshape(levels, piece, right.shape[1])
-        )
-
-    output_proj_grad = summed(cot_pair, attention_pair).T
-    query_proj_grad = summed(hidden_pair, query_pair)
-    kv_proj_grad = summed(hidden_pair, kv_pair)
+    halo_back = jnp.stack(
+        [
+            parts[(reach - offset) * tok_rows : (reach - offset + 1) * tok_rows].astype(BF16)
+            for offset in range(1, reach + 1)
+        ]
+    )
+    pair = jnp.concatenate([attention, query_grad], 1)
+    pair_near, kv_grad, kv_near = exchange(pair, parts[reach * tok_rows :], halo_back)
+
+    def summed(full, right, near, right_near):
+        own = transposed_dot(full, right).reshape(levels, 2, piece, right.shape[1])
+        own = jnp.where(parity == 0, own[:, 0], own[:, 1])
+        return (own + transposed_dot(near, right_near).reshape(own.shape)).astype(BF16)
+
+    q_width = query_grad.shape[1]
+    output_parts = summed(full_cotangent, attention, cot_near, pair_near[:, :q_width])
+    query_parts = summed(full_hidden, query_grad, hidden_near, pair_near[:, q_width:])
+    kv_parts = summed(full_hidden, kv_grad, hidden_near, kv_near)
 
     term = (
         right_transposed_dot(query_grad, query_proj)
         + right_transposed_dot(kv_grad[:, :kv_width], key_projection)
         + right_transposed_dot(kv_grad[:, kv_width:], value_projection)
     ).astype(BF16)
-    me = lax.axis_index("tp")
-    blocks = [term[:, i * shard_width : (i + 1) * shard_width] for i in range(tp_count)]
-    high, low = me // 2, me % 2
-    near = [
-        jnp.where(low == 0, blocks[2 * i], blocks[2 * i + 1]).astype(F32)
-        + swap(jnp.where(low == 0, blocks[2 * i + 1], blocks[2 * i]), "tp", 1).astype(F32)
-        for i in range(2)
-    ]
-    far = swap(jnp.where(high == 0, near[1], near[0]).astype(BF16), "tp", 2)
-    hidden_grad = (jnp.where(high == 0, near[0], near[1]) + far.astype(F32)).astype(BF16)
+    output_grad, query_proj_grad, kv_proj_grad, hidden_grad = final_sums(
+        output_parts, query_parts, kv_parts, term
+    )
     return (
         hidden_grad,
         query_proj_grad,
         kv_proj_grad[:, :kv_width],
         kv_proj_grad[:, kv_width:],
-        output_proj_grad,
+        output_grad.T,
     )
 
 

time: 247 us -> 229 us (0.927); the launches traced: 244 us -> 228 us
  Pallas kernels: 0 us -> 124 us
  waiting for transfers between devices: 99.6 us -> 27 us
  starting transfers between devices: 67.8 us -> 16.6 us
  other arithmetic: 31.8 us -> 22.2 us
  local copies, waits for them, and re-layouts: 16.6 us -> 7.81 us
  matrix products: 26.3 us -> 29.9 us
    pallas_call x0 -> x2, Pallas kernels: none -> 124 us  [the longest x1 67 us: final_sums(): pl.pallas_call(functools.partial(sum_kernel, levels), out_shape=[jax.Shap...]
    ppermute x18 -> x0, starting transfers between devices: 42.6 us -> none  [the longest x9 34.7 us: chain_sum(): up = lax.ppermute(up_value, 'seq', ups)]
    ppermute x20 -> x14, waiting for transfers between devices: 61.1 us -> 27 us  [swap(): return lax.ppermute(value, axis, [(i, i ^ bit) for i in range(count)])]
    ppermute x18 -> x0, waiting for transfers between devices: 33 us -> none  [the longest x9 16.7 us: chain_sum(): up = lax.ppermute(up_value, 'seq', ups)]
    concatenate x2 -> x0, local copies, waits for them, and re-layouts: 8.8 us -> none  [gather_features(): jnp.concatenate([jnp.where(low == 0, first, near_first), jnp.where(low ==...]
    dot_general x7 -> x10, matrix products: 7.27 us -> 12.8 us  [transposed_dot(): lax.dot_general(left, right, (((0,), (0,)), ((), ())), preferred_element_...]
    ppermute x4 -> x2, waiting for transfers between devices: 5.48 us -> 0.01 us  [shift(): lax.ppermute(value, 'seq', [(i, i + steps) for i in range(count) if 0 <=...]
    ppermute x20 -> x14, starting transfers between devices: 14.9 us -> 9.49 us  [swap(): return lax.ppermute(value, axis, [(i, i ^ bit) for i in range(count)])]
  transfers between devices with their start and end apart: 42 -> 16, of which waited for: 13 -> 3; matrix products, arithmetic and copies ran while one was open for 22% -> 21% of each run, Pallas kernels for 0% -> 25%
where the time goes in v2:
time: 229 us; the launch traced here: 228 us
  Pallas kernels  124 us (54%)
  matrix products  29.9 us (13%)
  waiting for transfers between devices  27 us (12%)
  other arithmetic  22.2 us (10%)
  starting transfers between devices  16.6 us (7%)
  local copies, waits for them, and re-layouts  7.81 us (3%)
    pallas_call x1, Pallas kernels, final_sums(): pl.pallas_call(functools.partial(sum_kernel, levels), out_shape=[jax.Shap...  67 us
    pallas_call x1, Pallas kernels, exchange(): pl.pallas_call(functools.partial(exchange_kernel, count, reach), out_shap...  56.5 us
    ppermute x14, waiting for transfers between devices, swap(): return lax.ppermute(value, axis, [(i, i ^ bit) for i in range(count)])  27 us
    dot_general x10, matrix products, transposed_dot(): lax.dot_general(left, right, (((0,), (0,)), ((), ())), preferred_element_...  12.8 us
    dot_general x8, matrix products, right_transposed_dot(): lax.dot_general(left, right, (((1,), (1,)), ((), ())), preferred_element_...  11.4 us
    ppermute x14, starting transfers between devices, swap(): return lax.ppermute(value, axis, [(i, i ^ bit) for i in range(count)])  9.49 us
    ppermute x2, starting transfers between devices, shift(): lax.ppermute(value, 'seq', [(i, i + steps) for i in range(count) if 0 <=...  7.12 us
    unnamed x39, local copies, waits for them, and re-layouts  6.85 us
  transfers between devices with their start and end apart: 16, of which 3 were waited for; matrix products, arithmetic and copies ran while one was open for 21% of the time, Pallas kernels for 25%

profile of v2, /device:TPU:0, one launch (start us, length us, event | category | flops | bytes accessed | tf_op | source)
XLA Modules:
  0.0 228.2 jit_solution(10484133502645492857)
XLA Ops:
  0.6 3.0 %collective-permute-start.5 = (bf16[512,640]{1,0:T(8,128)(2,1)}, bf16[512,640]{1,0:T(8,128)(2,1)}, u32[]{:S(2)}, u32[]{:S(2)}) collective-permute-start(bf16[512,640]{1,0:T(8,128)(2,1)} %param.7), channel_id=1, source_target_pairs={{0,2},{1,3},{2,0},{3,1},{4,6},{5,7},{6,4},{7,5},{8,10},{9,11},{10,... | collective-permute-start | bytes 1966088 | tf_op jit(solution)/shard_map/ppermute | solution.py:31
  3.7 1.3 copy.23
  5.1 14.4 %collective-permute-done.5 = bf16[512,640]{1,0:T(8,128)(2,1)} collective-permute-done((bf16[512,640]{1,0:T(8,128)(2,1)}, bf16[512,640]{1,0:T(8,128)(2,1)}, u32[]{:S(2)}, u32[]{:S(2)}) %collective-permute-start.5) | collective-permute-done | bytes 655392 | tf_op jit(solution)/shard_map/ppermute | solution.py:31
  19.5 2.5 %broadcast_select_fusion.1 = (bf16[512,640]{1,0:T(8,128)(2,1)}, bf16[512,640]{1,0:T(8,128)(2,1)}) fusion(bf16[512,640]{1,0:T(8,128)(2,1)} %param.7, bf16[512,640]{1,0:T(8,128)(2,1)} %collective-permute-done.5, pred[]{:T(512)S(6)} %eq.14), kind=kLoop, calls=%fused_computation.72 | loop fusion | flops 655360 | bytes 2621441 | tf_op jit(solution)/shard_map/jit(_where)/select_n | solution.py:45
  22.0 0.8 fusion.58
  22.8 2.1 collective-permute-start.3
  24.8 1.3 copy.24
  26.2 0.8 fusion.57
  27.2 5.6 %collective-permute-done = bf16[512,640]{1,0:T(8,128)(2,1)} collective-permute-done((bf16[512,640]{1,0:T(8,128)(2,1)}, bf16[512,640]{1,0:T(8,128)(2,1)}, u32[]{:S(2)}, u32[]{:S(2)}) %collective-permute-start) | collective-permute-done | bytes 655392 | tf_op jit(solution)/shard_map/ppermute | solution.py:31
  32.7 1.4 broadcast_select_fusion.3
  34.7 1.4 broadcast_select_fusion.5
  36.5 1.7 convolution_convert_fusion.1
  38.4 1.6 copy-done.15
  40.0 1.8 convolution_convert_fusion
  41.8 1.8 collective-permute-start.10
  43.6 1.5 fusion.36
  45.2 3.5 %collective-permute-start.9 = (bf16[512,512]{1,0:T(8,128)(2,1)S(1)}, bf16[512,512]{1,0:T(8,128)(2,1)S(1)}, u32[]{:S(2)}, u32[]{:S(2)}) collective-permute-start(bf16[512,512]{1,0:T(8,128)(2,1)S(1)} %fusion.36), channel_id=1, source_target_pairs={{0,4},{4,8},{8,12},{12,16},{16,20},{20,24},{24,28},{1,5},{5,9},{9,... | collective-permute-start | bytes 1572872 | tf_op jit(solution)/shard_map/ppermute | solution.py:36
  48.6 3.7 %collective-permute-start.8 = (bf16[512,512]{1,0:T(8,128)(2,1)S(1)}, bf16[512,512]{1,0:T(8,128)(2,1)S(1)}, u32[]{:S(2)}, u32[]{:S(2)}) collective-permute-start(bf16[512,512]{1,0:T(8,128)(2,1)S(1)} %fusion.36), channel_id=1, source_target_pairs={{0,8},{4,12},{8,16},{12,20},{16,24},{20,28},{1,9},{5,13},{9,17},{1... | collective-permute-start | bytes 1572872 | tf_op jit(solution)/shard_map/ppermute | solution.py:36
  52.9 1.0 broadcast_select_fusion.15
  54.5 6.9 %collective-permute-done.13 = bf16[512,320]{0,1:T(8,128)(2,1)S(1)} collective-permute-done((bf16[512,320]{0,1:T(8,128)(2,1)}, bf16[512,320]{0,1:T(8,128)(2,1)S(1)}, u32[]{:S(2)}, u32[]{:S(2)}) %collective-permute-start.13) | collective-permute-done | bytes 327712 | tf_op jit(solution)/shard_map/ppermute | solution.py:31
  61.4 1.0 broadcast_select_fusion.13
  63.2 1.2 fusion.84
  64.4 1.2 fusion.83
  68.5 0.7 multiply_reduce_fusion.1
  69.2 1.0 fusion.8
  72.1 1.0 fusion.9
  74.4 0.6 convolution_add_fusion
  75.3 1.8 fusion.40
  77.3 1.6 fusion.55
  79.1 56.5 %shard_map.110 = (bf16[512,1024]{1,0:T(8,128)(2,1)S(1)}, bf16[512,512]{1,0:T(8,128)(2,1)S(1)}, bf16[512,512]{1,0:T(8,128)(2,1)S(1)}) custom-call(bf16[512,1024]{1,0:T(8,128)(2,1)S(1)} %pad_maximum_fusion.5.pair, f32[512,512]{1,0:T(8,128)S(1)} %fusion.39.kv_own, bf16[2,512,512]{2,1,0:T(8,128)(2,1)S(1)} %pad_maximum_fusion.6.halo), custom_call_target="tpu_custom_call" | custom-call | tf_op jit(solution)/shard_map/pallas_call | solution.py:132
  135.5 2.9 %fusion.81 = f32[2560,512]{1,0:T(8,128)S(1)} fusion(bf16[512,512]{1,0:T(8,128)(2,1)S(1)} %get-tuple-element.21, bf16[512,640]{1,0:T(8,128)(2,1)S(1)} %copy-done.6, bf16[512,640]{1,0:T(8,128)(2,1)S(1)} %get-tuple-element.41, bf16[512,640]{1,0:T(8,128)(2,1)} %copy-done.9, bf16[512,640]{1,0:T(8,128)(2,1)} %copy-done.7), kind=kOutput, calls=%fused_computation.147 | convolution fusion | flops 1352663040 | bytes 8388608 | tf_op jit(solution)/shard_map/dot_general | solution.py:22
  138.4 0.9 fusion.60
  139.3 2.6 %add_convert_fusion.term = bf16[512,2560]{1,0:T(8,128)(2,1)} fusion(f32[512,2560]{1,0:T(8,128)S(1)} %fusion.55, f32[512,2560]{1,0:T(8,128)S(1)} %fusion.60, bf16[2560,256]{1,0:T(8,128)(2,1)S(1)} %copy-done.4, bf16[512,512]{1,0:T(8,128)(2,1)S(1)} %get-tuple-element.21), kind=kOutput, calls=%fused_computation | convolution fusion | flops 675020800 | bytes 14680064 | tf_op jit(solution)/shard_map/dot_general | solution.py:26
  142.0 1.6 fusion.56
  143.6 1.0 broadcast_select_fusion.17
  144.6 1.0 broadcast_select_fusion.19
  145.6 0.8 fusion.67
  146.5 1.0 broadcast_select_fusion.21
  147.5 2.4 %fusion.44 = f32[1280,512]{1,0:T(8,128)} fusion(bf16[512,1024]{1,0:T(8,128)(2,1)S(1)} %get-tuple-element.19, bf16[512,320]{0,1:T(8,128)(2,1)S(1)} %get-tuple-element.50, bf16[512,320]{0,1:T(8,128)(2,1)S(1)} %get-tuple-element.49, bf16[512,320]{0,1:T(8,128)(2,1)S(1)} %get-tuple-element.46, bf16[512,320]{0,1:T(8,128)(2,1)S(1)} %get-tuple-element.45), kind=kOutput, calls=%fused_computation.90 | convolution fusion | flops 676331520 | bytes 4456448 | tf_op jit(solution)/shard_map/dot_general | solution.py:22
  149.9 1.0 broadcast_select_fusion.23
  150.9 0.9 fusion.28
  151.8 1.1 fusion.21.parts_a
  152.8 4.9 %fusion.13 = (bf16[4,320,512]{2,1,0:T(8,128)(2,1)}, bf16[4,320,512]{2,1,0:T(8,128)(2,1)}) fusion(f32[4,320,512]{2,1,0:T(8,128)S(1)} %bitcast.99, f32[4,2,320,512]{3,2,1,0:T(8,128)S(1)} %bitcast.94, pred[]{:T(512)S(6)} %eq.12, f32[4,320,512]{2,1,0:T(8,128)} %bitcast.100, f32[4,2,320,512]{3,2,1,0:T(8,128)S(1)} %bitcast.95), kind=kLoop, calls=%fused_computation.29 | loop fusion | flops 3932160 | bytes 18350080 | tf_op jit(solution)/shard_map/convert_element_type | solution.py:399
  157.8 67.0 %shard_map.111 = (f32[320,512]{1,0:T(8,128)S(1)}, f32[320,512]{1,0:T(8,128)S(1)}, f32[320,512]{1,0:T(8,128)S(1)}, bf16[512,640]{1,0:T(8,128)(2,1)S(1)}) custom-call(bf16[4,320,512]{2,1,0:T(8,128)(2,1)S(1)} %fusion.21.parts_a, bf16[4,320,512]{2,1,0:T(8,128)(2,1)} %get-tuple-element.63.parts_b, bf16[4,320,512]{2,1,0:T(8,128)(2,1)} %get-tuple-element.62.parts_c, ...), custom_call_target="tpu_custom_call" | custom-call | tf_op jit(solution)/shard_map/pallas_call | solution.py:293
  224.8 0.9 fusion.82
  225.7 0.8 copy.56
  226.5 0.8 copy.57
  227.4 0.8 copy.58
  (80 shorter events, 9.7 us)
Async XLA Ops:
  0.6 35.9 %copy-start = (bf16[2560,512]{1,0:T(8,128)(2,1)S(1)}, bf16[2560,512]{1,0:T(8,128)(2,1)}, u32[]{:S(2)}) copy-start(bf16[2560,512]{1,0:T(8,128)(2,1)} %param.8) | copy-start | bytes 7864324
  0.6 18.9 %collective-permute-start.5 = (bf16[512,640]{1,0:T(8,128)(2,1)}, bf16[512,640]{1,0:T(8,128)(2,1)}, u32[]{:S(2)}, u32[]{:S(2)}) collective-permute-start(bf16[512,640]{1,0:T(8,128)(2,1)} %param.7), channel_id=1, source_target_pairs={{0,2},{1,3},{2,0},{3,1},{4,6},{5,7},{6,4},{7,5},{8,10},{9,11},{10,... | collective-permute-start | bytes 1966088 | tf_op jit(solution)/shard_map/ppermute | solution.py:31
  3.7 29.1 %collective-permute-start = (bf16[512,640]{1,0:T(8,128)(2,1)}, bf16[512,640]{1,0:T(8,128)(2,1)}, u32[]{:S(2)}, u32[]{:S(2)}) collective-permute-start(bf16[512,640]{1,0:T(8,128)(2,1)} %param.12), channel_id=1, source_target_pairs={{0,2},{1,3},{2,0},{3,1},{4,6},{5,7},{6,4},{7,5},{8,10},{9,11},{10,... | collective-permute-start | bytes 1966088 | tf_op jit(solution)/shard_map/ppermute | solution.py:31
  22.0 12.3 %collective-permute-start.7 = (bf16[512,640]{1,0:T(8,128)(2,1)}, bf16[512,640]{1,0:T(8,128)(2,1)}, u32[]{:S(2)}, u32[]{:S(2)}) collective-permute-start(bf16[512,640]{1,0:T(8,128)(2,1)} %get-tuple-element.40), channel_id=1, source_target_pairs={{0,1},{1,0},{2,3},{3,2},{4,5},{5,4},{6,7},{7,6},{8,9},{9,8},{10,11... | collective-permute-start | bytes 1966088 | tf_op jit(solution)/shard_map/ppermute | solution.py:31
  22.8 19.0 %collective-permute-start.3 = (bf16[512,320]{0,1:T(8,128)(2,1)}, bf16[512,320]{0,1:T(8,128)(2,1)}, u32[]{:S(2)}, u32[]{:S(2)}) collective-permute-start(bf16[512,320]{0,1:T(8,128)(2,1)} %fusion.58), channel_id=1, source_target_pairs={{0,4},{4,0},{8,12},{12,8},{16,20},{20,16},{24,28},{28,24},{1,5},{5... | collective-permute-start | bytes 983048 | tf_op jit(solution)/shard_map/ppermute | solution.py:31
  26.9 14.9 %collective-permute-start.4 = (bf16[512,320]{0,1:T(8,128)(2,1)}, bf16[512,320]{0,1:T(8,128)(2,1)}, u32[]{:S(2)}, u32[]{:S(2)}) collective-permute-start(bf16[512,320]{0,1:T(8,128)(2,1)} %fusion.57), channel_id=1, source_target_pairs={{0,4},{4,0},{8,12},{12,8},{16,20},{20,16},{24,28},{28,24},{1,5},{5... | collective-permute-start | bytes 983048 | tf_op jit(solution)/shard_map/ppermute | solution.py:31
  26.9 9.2 %copy-start.2 = (bf16[512,640]{1,0:T(8,128)(2,1)S(1)}, bf16[512,640]{1,0:T(8,128)(2,1)}, u32[]{:S(2)}) copy-start(bf16[512,640]{1,0:T(8,128)(2,1)} %get-tuple-element.39) | copy-start | bytes 1966084
  26.9 9.2 %collective-permute-start.6 = (bf16[512,640]{1,0:T(8,128)(2,1)}, bf16[512,640]{1,0:T(8,128)(2,1)S(1)}, u32[]{:S(2)}, u32[]{:S(2)}) collective-permute-start(bf16[512,640]{1,0:T(8,128)(2,1)} %get-tuple-element.39), channel_id=1, source_target_pairs={{0,1},{1,0},{2,3},{3,2},{4,5},{5,4},{6,7},{7,6},{8,9},{9,8},{10,11... | collective-permute-start | bytes 1966088 | tf_op jit(solution)/shard_map/ppermute | solution.py:31
  34.2 2.2 collective-permute-start.2
  34.3 4.0 %collective-permute-start.1 = (bf16[512,640]{1,0:T(8,128)(2,1)S(1)}, bf16[512,640]{1,0:T(8,128)(2,1)S(1)}, u32[]{:S(2)}, u32[]{:S(2)}) collective-permute-start(bf16[512,640]{1,0:T(8,128)(2,1)S(1)} %get-tuple-element.33), channel_id=1, source_target_pairs={{0,1},{1,0},{2,3},{3,2},{4,5},{5,4},{6,7},{7,6},{8,9},{9,8},{10,11... | collective-permute-start | bytes 1966088 | tf_op jit(solution)/shard_map/ppermute | solution.py:31
  36.2 7.5 %copy-start.5 = (bf16[512,640]{1,0:T(8,128)(2,1)}, bf16[512,640]{1,0:T(8,128)(2,1)S(1)}, u32[]{:S(2)}) copy-start(bf16[512,640]{1,0:T(8,128)(2,1)S(1)} %get-tuple-element.42) | copy-start | bytes 1966084
  36.3 7.3 %copy-start.7 = (bf16[512,640]{1,0:T(8,128)(2,1)}, bf16[512,640]{1,0:T(8,128)(2,1)S(1)}, u32[]{:S(2)}) copy-start(bf16[512,640]{1,0:T(8,128)(2,1)S(1)} %get-tuple-element.37) | copy-start | bytes 1966084
  36.3 7.3 %copy-start.9 = (bf16[512,640]{1,0:T(8,128)(2,1)}, bf16[512,640]{1,0:T(8,128)(2,1)S(1)}, u32[]{:S(2)}) copy-start(bf16[512,640]{1,0:T(8,128)(2,1)S(1)} %get-tuple-element.38) | copy-start | bytes 1966084
  38.3 1.7 copy-start.15
  40.0 3.6 %copy-start.3 = (bf16[2560,256]{1,0:T(8,128)(2,1)S(1)}, bf16[2560,256]{1,0:T(8,128)(2,1)}, u32[]{:S(2)}) copy-start(bf16[2560,256]{1,0:T(8,128)(2,1)} %param.9) | copy-start | bytes 3932164
  40.0 3.6 %copy-start.4 = (bf16[2560,256]{1,0:T(8,128)(2,1)S(1)}, bf16[2560,256]{1,0:T(8,128)(2,1)}, u32[]{:S(2)}) copy-start(bf16[2560,256]{1,0:T(8,128)(2,1)} %param.10) | copy-start | bytes 3932164
  41.8 11.1 %collective-permute-start.10 = (bf16[512,320]{0,1:T(8,128)(2,1)}, bf16[512,320]{0,1:T(8,128)(2,1)S(1)}, u32[]{:S(2)}, u32[]{:S(2)}) collective-permute-start(bf16[512,320]{0,1:T(8,128)(2,1)} %collective-permute-done.4), channel_id=1, source_target_pairs={{0,2},{1,3},{2,0},{3,1},{4,6},{5,7},{6,4},{7,5},{8,10},{9,11},{10,... | collective-permute-start | bytes 983048 | tf_op jit(solution)/shard_map/ppermute | solution.py:31
  45.2 17.4 %collective-permute-start.9 = (bf16[512,512]{1,0:T(8,128)(2,1)S(1)}, bf16[512,512]{1,0:T(8,128)(2,1)S(1)}, u32[]{:S(2)}, u32[]{:S(2)}) collective-permute-start(bf16[512,512]{1,0:T(8,128)(2,1)S(1)} %fusion.36), channel_id=1, source_target_pairs={{0,4},{4,8},{8,12},{12,16},{16,20},{20,24},{24,28},{1,5},{5,9},{9,... | collective-permute-start | bytes 1572872 | tf_op jit(solution)/shard_map/ppermute | solution.py:36
  48.6 14.4 %collective-permute-start.8 = (bf16[512,512]{1,0:T(8,128)(2,1)S(1)}, bf16[512,512]{1,0:T(8,128)(2,1)S(1)}, u32[]{:S(2)}, u32[]{:S(2)}) collective-permute-start(bf16[512,512]{1,0:T(8,128)(2,1)S(1)} %fusion.36), channel_id=1, source_target_pairs={{0,8},{4,12},{8,16},{12,20},{16,24},{20,28},{1,9},{5,13},{9,17},{1... | collective-permute-start | bytes 1572872 | tf_op jit(solution)/shard_map/ppermute | solution.py:36
  52.3 9.1 %collective-permute-start.13 = (bf16[512,320]{0,1:T(8,128)(2,1)}, bf16[512,320]{0,1:T(8,128)(2,1)S(1)}, u32[]{:S(2)}, u32[]{:S(2)}) collective-permute-start(bf16[512,320]{0,1:T(8,128)(2,1)} %collective-permute-done.3), channel_id=1, source_target_pairs={{0,2},{1,3},{2,0},{3,1},{4,6},{5,7},{6,4},{7,5},{8,10},{9,11},{10,... | collective-permute-start | bytes 983048 | tf_op jit(solution)/shard_map/ppermute | solution.py:31
  52.9 10.2 %copy-start.16 = (s32[512]{0:T(512)S(1)}, s32[512]{0:T(512)}, u32[]{:S(2)}) copy-start(s32[512]{0:T(512)} %param.13) | copy-start | bytes 6148
  53.9 92.5 %collective-permute-start.12 = (bf16[512,320]{0,1:T(8,128)(2,1)S(1)}, bf16[512,320]{0,1:T(8,128)(2,1)}, u32[]{:S(2)}, u32[]{:S(2)}) collective-permute-start(bf16[512,320]{0,1:T(8,128)(2,1)S(1)} %get-tuple-element.54), channel_id=1, source_target_pairs={{0,1},{1,0},{2,3},{3,2},{4,5},{5,4},{6,7},{7,6},{8,9},{9,8},{10,11... | collective-permute-start | bytes 983048 | tf_op jit(solution)/shard_map/ppermute | solution.py:31
  54.0 95.9 %collective-permute-start.11 = (bf16[512,320]{0,1:T(8,128)(2,1)S(1)}, bf16[512,320]{0,1:T(8,128)(2,1)}, u32[]{:S(2)}, u32[]{:S(2)}) collective-permute-start(bf16[512,320]{0,1:T(8,128)(2,1)S(1)} %get-tuple-element.53), channel_id=1, source_target_pairs={{0,1},{1,0},{2,3},{3,2},{4,5},{5,4},{6,7},{7,6},{8,9},{9,8},{10,11... | collective-permute-start | bytes 983048 | tf_op jit(solution)/shard_map/ppermute | solution.py:31
  62.5 81.1 %collective-permute-start.15 = (bf16[512,320]{0,1:T(8,128)(2,1)S(1)}, bf16[512,320]{0,1:T(8,128)(2,1)}, u32[]{:S(2)}, u32[]{:S(2)}) collective-permute-start(bf16[512,320]{0,1:T(8,128)(2,1)S(1)} %get-tuple-element.48), channel_id=1, source_target_pairs={{0,1},{1,0},{2,3},{3,2},{4,5},{5,4},{6,7},{7,6},{8,9},{9,8},{10,11... | collective-permute-start | bytes 983048 | tf_op jit(solution)/shard_map/ppermute | solution.py:31
  62.6 82.0 %collective-permute-start.14 = (bf16[512,320]{0,1:T(8,128)(2,1)S(1)}, bf16[512,320]{0,1:T(8,128)(2,1)}, u32[]{:S(2)}, u32[]{:S(2)}) collective-permute-start(bf16[512,320]{0,1:T(8,128)(2,1)S(1)} %get-tuple-element.47), channel_id=1, source_target_pairs={{0,1},{1,0},{2,3},{3,2},{4,5},{5,4},{6,7},{7,6},{8,9},{9,8},{10,11... | collective-permute-start | bytes 983048 | tf_op jit(solution)/shard_map/ppermute | solution.py:31
  70.9 6.4 %copy-start.11 = (bf16[512,256]{1,0:T(8,128)(2,1)}, bf16[512,256]{1,0:T(8,128)(2,1)S(1)}, u32[]{:S(2)}) copy-start(bf16[512,256]{1,0:T(8,128)(2,1)S(1)} %convolution_convert_fusion.2) | copy-start | bytes 786436
  73.8 3.5 %copy-start.13 = (bf16[512,256]{1,0:T(8,128)(2,1)}, bf16[512,256]{1,0:T(8,128)(2,1)S(1)}, u32[]{:S(2)}) copy-start(bf16[512,256]{1,0:T(8,128)(2,1)S(1)} %convolution_convert_fusion.3) | copy-start | bytes 786436
  79.0 56.5 %copy-start.6 = (bf16[512,640]{1,0:T(8,128)(2,1)S(1)}, bf16[512,640]{1,0:T(8,128)(2,1)}, u32[]{:S(2)}) copy-start(bf16[512,640]{1,0:T(8,128)(2,1)} %copy-done.5) | copy-start | bytes 1966084
  139.3 2.7 %copy-start.8 = (bf16[512,640]{1,0:T(8,128)(2,1)S(1)}, bf16[512,640]{1,0:T(8,128)(2,1)}, u32[]{:S(2)}) copy-start(bf16[512,640]{1,0:T(8,128)(2,1)} %copy-done.7) | copy-start | bytes 1966084
  139.3 2.7 %copy-start.10 = (bf16[512,640]{1,0:T(8,128)(2,1)S(1)}, bf16[512,640]{1,0:T(8,128)(2,1)}, u32[]{:S(2)}) copy-start(bf16[512,640]{1,0:T(8,128)(2,1)} %copy-done.9) | copy-start | bytes 1966084
  139.3 2.7 %copy-start.12 = (bf16[512,256]{1,0:T(8,128)(2,1)S(1)}, bf16[512,256]{1,0:T(8,128)(2,1)}, u32[]{:S(2)}) copy-start(bf16[512,256]{1,0:T(8,128)(2,1)} %copy-done.11) | copy-start | bytes 786436
  139.3 2.7 %copy-start.14 = (bf16[512,256]{1,0:T(8,128)(2,1)S(1)}, bf16[512,256]{1,0:T(8,128)(2,1)}, u32[]{:S(2)}) copy-start(bf16[512,256]{1,0:T(8,128)(2,1)} %copy-done.13) | copy-start | bytes 786436
  224.8 3.4 %copy-start.1 = (bf16[2560,512]{1,0:T(8,128)(2,1)S(1)}, bf16[2560,512]{1,0:T(8,128)(2,1)}, u32[]{:S(2)}) copy-start(bf16[2560,512]{1,0:T(8,128)(2,1)} %param.8) | copy-start | bytes 7864324

commit v3 on v2

--- a/solution.py
+++ b/solution.py
@@ -79,17 +79,33 @@
     pl.semaphore_wait(barrier, sum(jnp.where(here, 1, 0) for _, _, here in peers))
 
 
-def exchange_kernel(
-    count, reach, pair, kv_own, halo, pair_near, kv_grad, kv_near,
-    landed, total, swap_send, swap_recv, halo_send, halo_recv,
+def tail_kernel(
+    levels, count, reach,
+    attention, query_grad, kv_own, halo, own_t, near_t, cot_near_t, out_base, query_base,
+    term_base, kv_weights,
+    out_a, out_b, out_c, hidden,
+    near_data, landed, total, kv_grad, term, parts, up_tx, up_rx, down_tx, down_rx,
+    near_rx, far_tx, far_rx,
+    swap_send, swap_recv, halo_send, halo_recv,
+    up_send, up_recv, down_send, down_recv, hid_send, hid_recv,
 ):
+    outs = (out_a, out_b, out_c)
     me = lax.axis_index("seq")
-    near = me + 1 - 2 * lax.rem(me, 2)
-    peers = []
-    for offset in range(1, reach + 1):
+    z = me // 2
+    beside = me + 1 - 2 * lax.rem(me, 2)
+    tp = lax.axis_index("tp")
+    high, low = tp // 2, lax.rem(tp, 2)
+    near, far = tp + 1 - 2 * low, tp + 2 - 4 * high
+    width = hidden.shape[1]
+    always = tp >= 0
+    peers = [("tp", near, always), ("tp", far, always)]
+    for offset in range(1, max(reach, 2) + 1):
         peers.append(("seq", me - offset, me >= offset))
         peers.append(("seq", me + offset, me + offset < count))
     greet(pltpu.get_barrier_semaphore(), peers)
+
+    def columns(index):
+        return pl.ds(pl.multiple_of(index * width, width), width)
 
     def back(offset):
         return remote(
@@ -97,87 +113,10 @@
             halo_send.at[offset - 1], halo_recv.at[offset - 1], "seq", me - offset,
         )
 
-    for offset in range(reach, 0, -1):
-
-        @pl.when(me >= offset)
-        def _():
-            back(offset).start()
-
-    pair_copy = remote(pair, pair_near, swap_send.at[0], swap_recv.at[0], "seq", near)
-    pair_copy.start()
-    total[...] = kv_own[...]
-    for offset in range(reach, 0, -1):
-
-        @pl.when(me + offset < count)
-        def _():
-            back(offset).wait_recv()
-            total[...] += landed[offset - 1].astype(F32)
-
-    kv_grad[...] = total[...].astype(BF16)
-    kv_copy = remote(kv_grad, kv_near, swap_send.at[1], swap_recv.at[1], "seq", near)
-    kv_copy.start()
-    pair_copy.wait()
-    kv_copy.wait()
-    for offset in range(1, reach + 1):
-
-        @pl.when(me >= offset)
-        def _():
-            back(offset).wait_send()
-
-
-def exchange(pair, kv_own, halo):
-    count = lax.axis_size("seq")
-    reach = halo.shape[0]
-    vmem = pl.BlockSpec(memory_space=pltpu.VMEM)
-    return pl.pallas_call(
-        functools.partial(exchange_kernel, count, reach),
-        out_shape=[
-            jax.ShapeDtypeStruct(pair.shape, BF16),
-            jax.ShapeDtypeStruct(kv_own.shape, BF16),
-            jax.ShapeDtypeStruct(kv_own.shape, BF16),
-        ],
-        in_specs=[vmem] * 3,
-        out_specs=[vmem] * 3,
-        scratch_shapes=[
-            pltpu.VMEM(halo.shape, BF16),
-            pltpu.VMEM(kv_own.shape, F32),
-            pltpu.SemaphoreType.DMA((2,)),
-            pltpu.SemaphoreType.DMA((2,)),
-            pltpu.SemaphoreType.DMA((reach,)),
-            pltpu.SemaphoreType.DMA((reach,)),
-        ],
-        compiler_params=pltpu.CompilerParams(
-            collective_id=1, has_side_effects=True, vmem_limit_bytes=40 * 2**20
-        ),
-    )(pair, kv_own, halo)
-
-
-def sum_kernel(
-    levels, parts_a, parts_b, parts_c, term, out_a, out_b, out_c, hidden,
-    up_tx, up_rx, down_tx, down_rx, near_rx, far_tx, far_rx,
-    up_send, up_recv, down_send, down_recv, hid_send, hid_recv,
-):
-    parts = (parts_a, parts_b, parts_c)
-    outs = (out_a, out_b, out_c)
-    me = lax.axis_index("seq")
-    z = me // 2
-    tp = lax.axis_index("tp")
-    high, low = tp // 2, lax.rem(tp, 2)
-    near, far = tp + 1 - 2 * low, tp + 2 - 4 * high
-    width = hidden.shape[1]
-    always = tp >= 0
-    greet(
-        pltpu.get_barrier_semaphore(),
-        [
-            ("seq", me - 2, z >= 1),
-            ("seq", me + 2, z <= levels - 2),
-            ("tp", near, always),
-            ("tp", far, always),
-        ],
-    )
-
-    def columns(index):
-        return pl.ds(pl.multiple_of(index * width, width), width)
+    def swapped(slot, source):
+        return remote(
+            source, near_data.at[slot], swap_send.at[slot], swap_recv.at[slot], "seq", beside
+        )
 
     def near_copy(slot):
         half = 1 - high if slot == 0 else high
@@ -200,52 +139,113 @@
             down_send.at[step, c], down_recv.at[step, c], "seq", me - 2,
         )
 
+    def begin(c):
+        @pl.when(z == 0)
+        def _():
+            for step in range(levels - 1):
+                up_tx[step, c] = parts[c, levels - 1 - step]
+                up(step, c).start()
+
+        @pl.when(z == levels - 1)
+        def _():
+            for step in range(levels - 1):
+                down_tx[step, c] = parts[c, step]
+                down(step, c).start()
+
+    def advance(c, step):
+        gap = levels - 1 - step
+
+        @pl.when((z >= 1) & (z <= step))
+        def _():
+            up(step - 1, c).wait_recv()
+            up_tx[step, c] = (
+                parts[c, z + gap].astype(F32) + up_rx[step - 1, c].astype(F32)
+            ).astype(BF16)
+            up(step, c).start()
+
+        @pl.when((z >= gap) & (z <= levels - 2))
+        def _():
+            down(step - 1, c).wait_recv()
+            down_tx[step, c] = (
+                parts[c, z - gap].astype(F32) + down_rx[step - 1, c].astype(F32)
+            ).astype(BF16)
+            down(step, c).start()
+
+    def maybe_advance(c, step):
+        if step <= levels - 2:
+            advance(c, step)
+
+    def product(c, base, left, slot):
+        def body(b, carry):
+            parts[c, b] = (base[b] + dot(left[b], near_data[slot])).astype(BF16)
+            return carry
+
+        lax.fori_loop(0, levels, body, 0)
+
+    attention_copy = swapped(0, attention)
+    query_copy = swapped(1, query_grad)
+    kv_copy = swapped(2, kv_grad)
+    attention_copy.start()
+    for offset in range(reach, 0, -1):
+
+        @pl.when(me >= offset)
+        def _():
+            back(offset).start()
+
+    attention_copy.wait_recv()
+    query_copy.start()
+    product(0, out_base, cot_near_t, 0)
+    begin(0)
+    query_copy.wait_recv()
+    product(1, query_base, near_t, 1)
+    begin(1)
+    maybe_advance(0, 1)
+
+    total[...] = kv_own[...]
+    for offset in range(reach, 0, -1):
+
+        @pl.when(me + offset < count)
+        def _():
+            back(offset).wait_recv()
+            total[...] += landed[offset - 1].astype(F32)
+
+    kv_grad[...] = total[...].astype(BF16)
+    kv_copy.start()
+    maybe_advance(1, 1)
+
+    def term_body(i, carry):
+        rows = pl.ds(pl.multiple_of(i * width, width), width)
+        term[:, columns(i)] = (
+            term_base[:, columns(i)] + right_transposed_dot(kv_grad[...], kv_weights[rows, :])
+        ).astype(BF16)
+        return carry
+
+    lax.fori_loop(0, term.shape[1] // width, term_body, 0)
     near_copy(0).start()
     near_copy(1).start()
-    for step in range(levels - 1):
-        gap = levels - 1 - step
-        for c in range(3):
-
-            @pl.when(z <= step)
-            def _():
-                @pl.when(z == 0)
-                def _():
-                    up_tx[step, c] = parts[c][z + gap]
-
-                if step > 0:
-
-                    @pl.when(z >= 1)
-                    def _():
-                        up(step - 1, c).wait_recv()
-                        up_tx[step, c] = (
-                            parts[c][z + gap].astype(F32) + up_rx[step - 1, c].astype(F32)
-                        ).astype(BF16)
-
-                up(step, c).start()
-
-            @pl.when(z >= gap)
-            def _():
-                @pl.when(z == levels - 1)
-                def _():
-                    down_tx[step, c] = parts[c][z - gap]
-
-                if step > 0:
-
-                    @pl.when(z <= levels - 2)
-                    def _():
-                        down(step - 1, c).wait_recv()
-                        down_tx[step, c] = (
-                            parts[c][z - gap].astype(F32) + down_rx[step - 1, c].astype(F32)
-                        ).astype(BF16)
-
-                down(step, c).start()
-
-        if step == 0:
-            near_copy(0).wait_recv()
-            far_tx[...] = (
-                term[:, columns(2 * (1 - high) + low)].astype(F32) + near_rx[0].astype(F32)
-            ).astype(BF16)
-            far_copy.start()
+
+    maybe_advance(0, 2)
+    kv_copy.wait_recv()
+
+    def kv_body(b, carry):
+        parts[2, b] = (
+            dot(own_t[b], kv_grad[...]) + dot(near_t[b], near_data[2])
+        ).astype(BF16)
+        return carry
+
+    lax.fori_loop(0, levels, kv_body, 0)
+    begin(2)
+    maybe_advance(1, 2)
+    near_copy(0).wait_recv()
+    far_tx[...] = (
+        term[:, columns(2 * (1 - high) + low)].astype(F32) + near_rx[0].astype(F32)
+    ).astype(BF16)
+    far_copy.start()
+    for step in range(3, levels - 1):
+        advance(0, step)
+        advance(1, step)
+    for step in range(1, levels - 1):
+        advance(2, step)
     near_copy(1).wait_recv()
     far_copy.wait_recv()
     hidden[...] = (
@@ -255,7 +255,7 @@
     ).astype(BF16)
     last = levels - 2
     for c in range(3):
-        outs[c][...] = parts[c][z].astype(F32)
+        outs[c][...] = parts[c, z].astype(F32)
 
         @pl.when(z >= 1)
         def _():
@@ -266,6 +266,15 @@
         def _():
             down(last, c).wait_recv()
             outs[c][...] += down_rx[last, c].astype(F32)
+
+    attention_copy.wait_send()
+    query_copy.wait_send()
+    kv_copy.wait_send()
+    for offset in range(1, reach + 1):
+
+        @pl.when(me >= offset)
+        def _():
+            back(offset).wait_send()
 
     near_copy(0).wait_send()
     near_copy(1).wait_send()
@@ -282,33 +291,44 @@
                 down(step, c).wait_send()
 
 
-def final_sums(parts_a, parts_b, parts_c, term):
-    levels, rows, columns = parts_a.shape
-    shard = term.shape[1] // lax.axis_size("tp")
+def tail(attention, query_grad, kv_own, halo, own_t, near_t, cot_near_t, out_base, query_base,
+         term_base, kv_weights):
+    levels, rows, tokens = own_t.shape
+    columns = attention.shape[1]
+    count = lax.axis_size("seq")
+    reach = halo.shape[0]
+    shard = term_base.shape[1] // lax.axis_size("tp")
     vmem = pl.BlockSpec(memory_space=pltpu.VMEM)
     steps = levels - 1
     slots = pltpu.VMEM((steps, 3, rows, columns), BF16)
-    block = (term.shape[0], shard)
+    block = (tokens, shard)
     sems = pltpu.SemaphoreType.DMA((steps, 3))
+    three = pltpu.SemaphoreType.DMA((3,))
+    some = pltpu.SemaphoreType.DMA((reach,))
     return pl.pallas_call(
-        functools.partial(sum_kernel, levels),
+        functools.partial(tail_kernel, levels, count, reach),
         out_shape=[jax.ShapeDtypeStruct((rows, columns), F32)] * 3
         + [jax.ShapeDtypeStruct(block, BF16)],
-        in_specs=[vmem] * 4,
+        in_specs=[vmem] * 11,
         out_specs=[vmem] * 4,
         scratch_shapes=[
+            pltpu.VMEM((3,) + attention.shape, BF16),
+            pltpu.VMEM(halo.shape, BF16),
+            pltpu.VMEM(kv_own.shape, F32),
+            pltpu.VMEM(kv_own.shape, BF16),
+            pltpu.VMEM(term_base.shape, BF16),
+            pltpu.VMEM((3, levels, rows, columns), BF16),
             slots, slots, slots, slots,
             pltpu.VMEM((2,) + block, BF16),
             pltpu.VMEM(block, BF16),
             pltpu.VMEM(block, BF16),
-            sems, sems, sems, sems,
-            pltpu.SemaphoreType.DMA((3,)),
-            pltpu.SemaphoreType.DMA((3,)),
+            three, three, some, some, sems, sems, sems, sems, three, three,
         ],
         compiler_params=pltpu.CompilerParams(
-            collective_id=2, has_side_effects=True, vmem_limit_bytes=50 * 2**20
+            collective_id=1, has_side_effects=True, vmem_limit_bytes=56 * 2**20
         ),
-    )(parts_a, parts_b, parts_c, term)
+    )(attention, query_grad, kv_own, halo, own_t, near_t, cot_near_t, out_base, query_base,
+      term_base, kv_weights)
 
 
 def per_device(
@@ -331,7 +351,8 @@
         return jnp.where(parity == 0, odd, even)
 
     full_hidden = gather_features(hidden_in)
-    key_values = dot(full_hidden, jnp.concatenate([key_projection, value_projection], 1)).astype(BF16)
+    kv_weights = jnp.concatenate([key_projection, value_projection], 1)
+    key_values = dot(full_hidden, kv_weights).astype(BF16)
     halo = [shift(key_values, offset) for offset in range(1, reach + 1)]
     full_cotangent = gather_features(out_cotangent)
     query_matrix = dot(full_hidden, query_proj).astype(BF16)
@@ -390,26 +411,26 @@
             for offset in range(1, reach + 1)
         ]
     )
-    pair = jnp.concatenate([attention, query_grad], 1)
-    pair_near, kv_grad, kv_near = exchange(pair, parts[reach * tok_rows :], halo_back)
-
-    def summed(full, right, near, right_near):
-        own = transposed_dot(full, right).reshape(levels, 2, piece, right.shape[1])
-        own = jnp.where(parity == 0, own[:, 0], own[:, 1])
-        return (own + transposed_dot(near, right_near).reshape(own.shape)).astype(BF16)
-
-    q_width = query_grad.shape[1]
-    output_parts = summed(full_cotangent, attention, cot_near, pair_near[:, :q_width])
-    query_parts = summed(full_hidden, query_grad, hidden_near, pair_near[:, q_width:])
-    kv_parts = summed(full_hidden, kv_grad, hidden_near, kv_near)
-
-    term = (
-        right_transposed_dot(query_grad, query_proj)
-        + right_transposed_dot(kv_grad[:, :kv_width], key_projection)
-        + right_transposed_dot(kv_grad[:, kv_width:], value_projection)
-    ).astype(BF16)
-    output_grad, query_proj_grad, kv_proj_grad, hidden_grad = final_sums(
-        output_parts, query_parts, kv_parts, term
+
+    def own_rows(array):
+        split = array.reshape(levels, 2, piece, array.shape[1])
+        return jnp.where(parity == 0, split[:, 0], split[:, 1])
+
+    def near_rows(array):
+        return array.T.reshape(levels, piece, tok_rows)
+
+    output_grad, query_proj_grad, kv_proj_grad, hidden_grad = tail(
+        attention,
+        query_grad,
+        parts[reach * tok_rows :],
+        halo_back,
+        own_rows(full_hidden.T),
+        near_rows(hidden_near),
+        near_rows(cot_near),
+        own_rows(transposed_dot(full_cotangent, attention)),
+        own_rows(transposed_dot(full_hidden, query_grad)),
+        right_transposed_dot(query_grad, query_proj),
+        kv_weights,
     )
     return (
         hidden_grad,

time: 229 us -> 210 us (0.917)
  Pallas kernels: 124 us -> 108 us
  matrix products: 29.9 us -> 21.5 us
  local copies, waits for them, and re-layouts: 7.81 us -> 12.7 us
    pallas_call x2 -> x1, Pallas kernels: 124 us -> 108 us  [tail(): pl.pallas_call(functools.partial(tail_kernel, levels, count, reach), out_...]
    dot_general x10 -> x6, matrix products: 12.8 us -> 5.49 us  [transposed_dot(): lax.dot_general(left, right, (((0,), (0,)), ((), ())), preferred_element_...]
    convert_element_type x2 -> x0, other arithmetic: 5.97 us -> none  [summed(): (own + transposed_dot(near, right_near).reshape(own.shape)).astype(BF16)]
    select_n x0 -> x2, other arithmetic: none -> 5.25 us  [own_rows(): return jnp.where(parity == 0, split[:, 0], split[:, 1])]
    unnamed x39 -> x22, local copies, waits for them, and re-layouts: 6.85 us -> 10.4 us
    concatenate x1 -> x4, other arithmetic: 0.13 us -> 3.61 us  [the longest x3 2.57 us: gather_features(): jnp.concatenate([jnp.where(low == 0, first, near_first), jnp.where(low ==...]
    select_n x4, other arithmetic: 3.59 us -> 0.28 us  [gather_features(): jnp.where(low == 0, second, near_second)]
    dot_general x8 -> x6, matrix products: 11.4 us -> 10.5 us  [right_transposed_dot(): lax.dot_general(left, right, (((1,), (1,)), ((), ())), preferred_element_...]
  transfers between devices with their start and end apart: 16 -> 16, of which waited for: 3 -> 5; matrix products, arithmetic and copies ran while one was open for 21% -> 22% of each run, Pallas kernels for 25% -> 0%
where the time goes in v3:
time: 210 us
  Pallas kernels  108 us (51%)
  waiting for transfers between devices  28.4 us (14%)
  matrix products  21.5 us (10%)
  other arithmetic  21.3 us (10%)
  starting transfers between devices  16.8 us (8%)
  local copies, waits for them, and re-layouts  12.7 us (6%)
    pallas_call x1, Pallas kernels, tail(): pl.pallas_call(functools.partial(tail_kernel, levels, count, reach), out_...  108 us
    ppermute x14, waiting for transfers between devices, swap(): return lax.ppermute(value, axis, [(i, i ^ bit) for i in range(count)])  28.4 us
    dot_general x6, matrix products, right_transposed_dot(): lax.dot_general(left, right, (((1,), (1,)), ((), ())), preferred_element_...  10.5 us
    unnamed x22, local copies, waits for them, and re-layouts  10.4 us
    ppermute x14, starting transfers between devices, swap(): return lax.ppermute(value, axis, [(i, i ^ bit) for i in range(count)])  9.69 us
    ppermute x2, starting transfers between devices, shift(): lax.ppermute(value, 'seq', [(i, i + steps) for i in range(count) if 0 <=...  7.12 us
    dot_general x6, matrix products, dot(): return jnp.dot(left, right, preferred_element_type=F32)  5.51 us
    dot_general x6, matrix products, transposed_dot(): lax.dot_general(left, right, (((0,), (0,)), ((), ())), preferred_element_...  5.49 us
  transfers between devices with their start and end apart: 16, of which 5 were waited for; matrix products, arithmetic and copies ran while one was open for 22% of the time, Pallas kernels for 0%

profile of v3, /device:TPU:0, one launch (start us, length us, event | category | flops | bytes accessed | tf_op | source)
XLA Modules:
  0.0 209.7 jit_solution(1972818710101631356)
XLA Ops:
  0.6 1.5 copy.24
  2.1 3.0 %collective-permute-start.2 = (bf16[512,640]{0,1:T(8,128)(2,1)S(1)}, bf16[512,640]{0,1:T(8,128)(2,1)}, u32[]{:S(2)}, u32[]{:S(2)}) collective-permute-start(bf16[512,640]{0,1:T(8,128)(2,1)S(1)} %copy.24), channel_id=1, source_target_pairs={{0,2},{1,3},{2,0},{3,1},{4,6},{5,7},{6,4},{7,5},{8,10},{9,11},{10,... | collective-permute-start | bytes 1966088 | tf_op jit(solution)/shard_map/ppermute | solution.py:31
  5.1 0.8 fusion.29
  5.9 1.5 collective-permute-start
  7.4 2.2 %copy.25 = bf16[512,640]{0,1:T(8,128)(2,1)} copy(bf16[512,640]{1,0:T(8,128)(2,1)} %param.12) | data formatting | bytes 1310720 | tf_op args[5]
  10.1 1.8 fusion.28
  12.0 1.5 constant_dynamic-update-slice_fusion.1
  13.5 20.6 %collective-permute-done.5 = bf16[512,640]{0,1:T(8,128)(2,1)} collective-permute-done((bf16[512,640]{0,1:T(8,128)(2,1)}, bf16[512,640]{0,1:T(8,128)(2,1)}, u32[]{:S(2)}, u32[]{:S(2)}) %collective-permute-start.5) | collective-permute-done | bytes 655392 | tf_op jit(solution)/shard_map/ppermute | solution.py:31
  34.0 1.2 broadcast_select_fusion.1
  35.3 1.2 broadcast_select_fusion.3
  37.8 0.9 collective-permute-done.3
  38.9 0.8 collective-permute-done.4
  39.8 1.5 convolution_convert_fusion.2
  41.5 1.6 copy-done.6
  43.1 1.8 convolution_convert_fusion.1
  44.9 1.8 collective-permute-start.10
  46.8 1.5 convolution_convert_fusion
  48.5 3.5 %collective-permute-start.9 = (bf16[512,512]{1,0:T(8,128)(2,1)S(1)}, bf16[512,512]{1,0:T(8,128)(2,1)S(1)}, u32[]{:S(2)}, u32[]{:S(2)}) collective-permute-start(bf16[512,512]{1,0:T(8,128)(2,1)S(1)} %convolution_convert_fusion), channel_id=1, source_target_pairs={{0,4},{4,8},{8,12},{12,16},{16,20},{20,24},{24,28},{1,5},{5,9},{9,... | collective-permute-start | bytes 1572872 | tf_op jit(solution)/shard_map/ppermute | solution.py:36
  52.0 3.7 %collective-permute-start.8 = (bf16[512,512]{1,0:T(8,128)(2,1)S(1)}, bf16[512,512]{1,0:T(8,128)(2,1)S(1)}, u32[]{:S(2)}, u32[]{:S(2)}) collective-permute-start(bf16[512,512]{1,0:T(8,128)(2,1)S(1)} %convolution_convert_fusion), channel_id=1, source_target_pairs={{0,8},{4,12},{8,16},{12,20},{16,24},{20,28},{1,9},{5,13},{9,17},{1... | collective-permute-start | bytes 1572872 | tf_op jit(solution)/shard_map/ppermute | solution.py:36
  55.7 0.6 collective-permute-start.13
  56.3 1.2 fusion.17.own_t
  57.5 1.0 broadcast_select_fusion.15
  59.1 6.0 %collective-permute-done.13 = bf16[512,320]{0,1:T(8,128)(2,1)S(1)} collective-permute-done((bf16[512,320]{0,1:T(8,128)(2,1)}, bf16[512,320]{0,1:T(8,128)(2,1)S(1)}, u32[]{:S(2)}, u32[]{:S(2)}) %collective-permute-start.13) | collective-permute-done | bytes 327712 | tf_op jit(solution)/shard_map/ppermute | solution.py:31
  65.1 1.0 broadcast_select_fusion.13
  66.8 1.2 fusion.45
  68.1 1.2 fusion.46
  70.5 0.6 convolution_convert_fusion.5
  71.1 0.6 fusion.35
  72.8 0.7 multiply_reduce_fusion.1
  73.5 1.0 fusion.8
  75.1 0.6 fusion.30
  75.7 1.1 fusion.9
  77.4 1.5 fusion.43
  78.9 4.1 %fusion.42.term_base = f32[512,2560]{1,0:T(8,128)} fusion(bf16[2560,512]{1,0:T(8,128)(2,1)S(1)} %copy-done, bf16[512,256]{1,0:T(8,128)(2,1)S(1)} %convolution_convert_fusion.3, bf16[512,256]{1,0:T(8,128)(2,1)S(1)} %convolution_convert_fusion.4), kind=kOutput, calls=%fused_computation.113 | convolution fusion | flops 1343225856 | bytes 8388608 | tf_op jit(solution)/shard_map/dot_general | solution.py:26
  83.0 0.6 convolution_add_fusion
  83.6 0.6 convolution_add_fusion.1
  84.5 1.5 fusion.27
  86.0 4.1 %fusion.11 = (f32[4,320,512]{2,1,0:T(8,128)}, f32[4,320,512]{2,1,0:T(8,128)}) fusion(f32[4,2,320,512]{3,2,1,0:T(8,128)S(1)} %bitcast.75, pred[]{:T(512)S(6)} %eq.12, f32[4,2,320,512]{3,2,1,0:T(8,128)S(1)} %bitcast.76), kind=kLoop, calls=%fused_computation.26 | loop fusion | flops 1310720 | bytes 15728641 | tf_op jit(solution)/shard_map/jit(_where)/select_n | solution.py:417
  90.1 1.1 fusion.18.kv_own
  91.2 1.0 pad_maximum_fusion.7
  92.3 1.1 pad_maximum_fusion.6.halo
  93.5 1.2 pad_maximum_fusion.4
  94.8 1.2 pad_maximum_fusion.5
  95.9 108.1 %shard_map.110 = (f32[320,512]{1,0:T(8,128)}, f32[320,512]{1,0:T(8,128)}, f32[320,512]{1,0:T(8,128)}, bf16[512,640]{1,0:T(8,128)(2,1)}) custom-call(bf16[512,512]{1,0:T(8,128)(2,1)} %get-tuple-element.58.attention, bf16[512,512]{1,0:T(8,128)(2,1)} %get-tuple-element.59.query_grad, f32[512,512]{1,0:T(8,128)} %fusion.18.kv_own, ...), custom_call_target="tpu_custom_call" | custom-call | tf_op jit(solution)/shard_map/pallas_call | solution.py:308
  204.0 2.0 fusion.44
  206.1 2.0 copy.64
  208.0 0.8 copy.65
  208.9 0.8 copy.66
  (60 shorter events, 7.7 us)
Async XLA Ops:
  0.6 39.2 %copy-start = (bf16[2560,512]{1,0:T(8,128)(2,1)S(1)}, bf16[2560,512]{1,0:T(8,128)(2,1)}, u32[]{:S(2)}) copy-start(bf16[2560,512]{1,0:T(8,128)(2,1)} %param.8) | copy-start | bytes 7864324
  2.1 33.2 %collective-permute-start.2 = (bf16[512,640]{0,1:T(8,128)(2,1)S(1)}, bf16[512,640]{0,1:T(8,128)(2,1)}, u32[]{:S(2)}, u32[]{:S(2)}) collective-permute-start(bf16[512,640]{0,1:T(8,128)(2,1)S(1)} %copy.24), channel_id=1, source_target_pairs={{0,2},{1,3},{2,0},{3,1},{4,6},{5,7},{6,4},{7,5},{8,10},{9,11},{10,... | collective-permute-start | bytes 1966088 | tf_op jit(solution)/shard_map/ppermute | solution.py:31
  5.9 39.0 %collective-permute-start = (bf16[512,320]{0,1:T(8,128)(2,1)}, bf16[512,320]{0,1:T(8,128)(2,1)}, u32[]{:S(2)}, u32[]{:S(2)}) collective-permute-start(bf16[512,320]{0,1:T(8,128)(2,1)} %fusion.29), channel_id=1, source_target_pairs={{0,4},{4,0},{8,12},{12,8},{16,20},{20,16},{24,28},{28,24},{1,5},{5... | collective-permute-start | bytes 983048 | tf_op jit(solution)/shard_map/ppermute | solution.py:31
  9.6 24.4 %collective-permute-start.5 = (bf16[512,640]{0,1:T(8,128)(2,1)}, bf16[512,640]{0,1:T(8,128)(2,1)}, u32[]{:S(2)}, u32[]{:S(2)}) collective-permute-start(bf16[512,640]{0,1:T(8,128)(2,1)} %copy.25), channel_id=1, source_target_pairs={{0,2},{1,3},{2,0},{3,1},{4,6},{5,7},{6,4},{7,5},{8,10},{9,11},{10,... | collective-permute-start | bytes 1966088 | tf_op jit(solution)/shard_map/ppermute | solution.py:31
  11.9 33.0 %collective-permute-start.1 = (bf16[512,320]{0,1:T(8,128)(2,1)}, bf16[512,320]{0,1:T(8,128)(2,1)}, u32[]{:S(2)}, u32[]{:S(2)}) collective-permute-start(bf16[512,320]{0,1:T(8,128)(2,1)} %fusion.28), channel_id=1, source_target_pairs={{0,4},{4,0},{8,12},{12,8},{16,20},{20,16},{24,28},{28,24},{1,5},{5... | collective-permute-start | bytes 983048 | tf_op jit(solution)/shard_map/ppermute | solution.py:31
  12.0 22.1 %copy-start.2 = (bf16[512,640]{0,1:T(8,128)(2,1)S(1)}, bf16[512,640]{0,1:T(8,128)(2,1)}, u32[]{:S(2)}) copy-start(bf16[512,640]{0,1:T(8,128)(2,1)} %copy.25) | copy-start | bytes 1966084
  13.4 23.6 %copy-start.3 = (bf16[2560,256]{1,0:T(8,128)(2,1)S(1)}, bf16[2560,256]{1,0:T(8,128)(2,1)}, u32[]{:S(2)}) copy-start(bf16[2560,256]{1,0:T(8,128)(2,1)} %param.10) | copy-start | bytes 3932164
  35.2 2.2 %collective-permute-start.6 = (bf16[512,640]{0,1:T(8,128)(2,1)S(1)}, bf16[512,640]{0,1:T(8,128)(2,1)S(1)}, u32[]{:S(2)}, u32[]{:S(2)}) collective-permute-start(bf16[512,640]{0,1:T(8,128)(2,1)S(1)} %get-tuple-element.27), channel_id=1, source_target_pairs={{0,1},{1,0},{2,3},{3,2},{4,5},{5,4},{6,7},{7,6},{8,9},{9,8},{10,11... | collective-permute-start | bytes 1966088 | tf_op jit(solution)/shard_map/ppermute | solution.py:31
  36.5 2.3 %collective-permute-start.3 = (bf16[512,640]{0,1:T(8,128)(2,1)S(1)}, bf16[512,640]{0,1:T(8,128)(2,1)S(1)}, u32[]{:S(2)}, u32[]{:S(2)}) collective-permute-start(bf16[512,640]{0,1:T(8,128)(2,1)S(1)} %get-tuple-element.33), channel_id=1, source_target_pairs={{0,1},{1,0},{2,3},{3,2},{4,5},{5,4},{6,7},{7,6},{8,9},{9,8},{10,11... | collective-permute-start | bytes 1966088 | tf_op jit(solution)/shard_map/ppermute | solution.py:31
  37.1 9.6 %copy-start.1 = (bf16[2560,512]{1,0:T(8,128)(2,1)}, bf16[2560,512]{1,0:T(8,128)(2,1)S(1)}, u32[]{:S(2)}) copy-start(bf16[2560,512]{1,0:T(8,128)(2,1)S(1)} %constant_dynamic-update-slice_fusion.kv_weights) | copy-start | bytes 7864324
  37.1 2.5 %collective-permute-start.4 = (bf16[512,640]{0,1:T(8,128)(2,1)S(1)}, bf16[512,640]{0,1:T(8,128)(2,1)S(1)}, u32[]{:S(2)}, u32[]{:S(2)}) collective-permute-start(bf16[512,640]{0,1:T(8,128)(2,1)S(1)} %get-tuple-element.34), channel_id=1, source_target_pairs={{0,1},{1,0},{2,3},{3,2},{4,5},{5,4},{6,7},{7,6},{8,9},{9,8},{10,11... | collective-permute-start | bytes 1966088 | tf_op jit(solution)/shard_map/ppermute | solution.py:31
  37.4 4.0 %collective-permute-start.7 = (bf16[512,640]{0,1:T(8,128)(2,1)S(1)}, bf16[512,640]{0,1:T(8,128)(2,1)S(1)}, u32[]{:S(2)}, u32[]{:S(2)}) collective-permute-start(bf16[512,640]{0,1:T(8,128)(2,1)S(1)} %get-tuple-element.28), channel_id=1, source_target_pairs={{0,1},{1,0},{2,3},{3,2},{4,5},{5,4},{6,7},{7,6},{8,9},{9,8},{10,11... | collective-permute-start | bytes 1966088 | tf_op jit(solution)/shard_map/ppermute | solution.py:31
  41.3 1.7 copy-start.6
  44.9 12.5 %collective-permute-start.10 = (bf16[512,320]{0,1:T(8,128)(2,1)}, bf16[512,320]{0,1:T(8,128)(2,1)S(1)}, u32[]{:S(2)}, u32[]{:S(2)}) collective-permute-start(bf16[512,320]{0,1:T(8,128)(2,1)} %collective-permute-done), channel_id=1, source_target_pairs={{0,2},{1,3},{2,0},{3,1},{4,6},{5,7},{6,4},{7,5},{8,10},{9,11},{10,... | collective-permute-start | bytes 983048 | tf_op jit(solution)/shard_map/ppermute | solution.py:31
  48.5 17.7 %collective-permute-start.9 = (bf16[512,512]{1,0:T(8,128)(2,1)S(1)}, bf16[512,512]{1,0:T(8,128)(2,1)S(1)}, u32[]{:S(2)}, u32[]{:S(2)}) collective-permute-start(bf16[512,512]{1,0:T(8,128)(2,1)S(1)} %convolution_convert_fusion), channel_id=1, source_target_pairs={{0,4},{4,8},{8,12},{12,16},{16,20},{20,24},{24,28},{1,5},{5,9},{9,... | collective-permute-start | bytes 1572872 | tf_op jit(solution)/shard_map/ppermute | solution.py:36
  52.0 14.7 %collective-permute-start.8 = (bf16[512,512]{1,0:T(8,128)(2,1)S(1)}, bf16[512,512]{1,0:T(8,128)(2,1)S(1)}, u32[]{:S(2)}, u32[]{:S(2)}) collective-permute-start(bf16[512,512]{1,0:T(8,128)(2,1)S(1)} %convolution_convert_fusion), channel_id=1, source_target_pairs={{0,8},{4,12},{8,16},{12,20},{16,24},{20,28},{1,9},{5,13},{9,17},{1... | collective-permute-start | bytes 1572872 | tf_op jit(solution)/shard_map/ppermute | solution.py:36
  55.7 9.4 %collective-permute-start.13 = (bf16[512,320]{0,1:T(8,128)(2,1)}, bf16[512,320]{0,1:T(8,128)(2,1)S(1)}, u32[]{:S(2)}, u32[]{:S(2)}) collective-permute-start(bf16[512,320]{0,1:T(8,128)(2,1)} %collective-permute-done.1), channel_id=1, source_target_pairs={{0,2},{1,3},{2,0},{3,1},{4,6},{5,7},{6,4},{7,5},{8,10},{9,11},{10,... | collective-permute-start | bytes 983048 | tf_op jit(solution)/shard_map/ppermute | solution.py:31
  57.5 9.3 %copy-start.7 = (s32[512]{0:T(512)S(1)}, s32[512]{0:T(512)}, u32[]{:S(2)}) copy-start(s32[512]{0:T(512)} %param.13) | copy-start | bytes 6148
  58.5 34.8 %collective-permute-start.11 = (bf16[512,320]{0,1:T(8,128)(2,1)S(1)}, bf16[512,320]{0,1:T(8,128)(2,1)S(1)}, u32[]{:S(2)}, u32[]{:S(2)}) collective-permute-start(bf16[512,320]{0,1:T(8,128)(2,1)S(1)} %get-tuple-element.47), channel_id=1, source_target_pairs={{0,1},{1,0},{2,3},{3,2},{4,5},{5,4},{6,7},{7,6},{8,9},{9,8},{10,11... | collective-permute-start | bytes 983048 | tf_op jit(solution)/shard_map/ppermute | solution.py:31
  58.6 34.8 %collective-permute-start.12 = (bf16[512,320]{0,1:T(8,128)(2,1)S(1)}, bf16[512,320]{0,1:T(8,128)(2,1)S(1)}, u32[]{:S(2)}, u32[]{:S(2)}) collective-permute-start(bf16[512,320]{0,1:T(8,128)(2,1)S(1)} %get-tuple-element.48), channel_id=1, source_target_pairs={{0,1},{1,0},{2,3},{3,2},{4,5},{5,4},{6,7},{7,6},{8,9},{9,8},{10,11... | collective-permute-start | bytes 983048 | tf_op jit(solution)/shard_map/ppermute | solution.py:31
  66.1 27.3 %collective-permute-start.14 = (bf16[512,320]{0,1:T(8,128)(2,1)S(1)}, bf16[512,320]{0,1:T(8,128)(2,1)S(1)}, u32[]{:S(2)}, u32[]{:S(2)}) collective-permute-start(bf16[512,320]{0,1:T(8,128)(2,1)S(1)} %get-tuple-element.41), channel_id=1, source_target_pairs={{0,1},{1,0},{2,3},{3,2},{4,5},{5,4},{6,7},{7,6},{8,9},{9,8},{10,11... | collective-permute-start | bytes 983048 | tf_op jit(solution)/shard_map/ppermute | solution.py:31
  66.2 28.5 %collective-permute-start.15 = (bf16[512,320]{0,1:T(8,128)(2,1)S(1)}, bf16[512,320]{0,1:T(8,128)(2,1)S(1)}, u32[]{:S(2)}, u32[]{:S(2)}) collective-permute-start(bf16[512,320]{0,1:T(8,128)(2,1)S(1)} %get-tuple-element.42), channel_id=1, source_target_pairs={{0,1},{1,0},{2,3},{3,2},{4,5},{5,4},{6,7},{7,6},{8,9},{9,8},{10,11... | collective-permute-start | bytes 983048 | tf_op jit(solution)/shard_map/ppermute | solution.py:31
  204.0 4.1 %copy-start.5 = (f32[320,512]{1,0:T(8,128)S(1)}, f32[320,512]{1,0:T(8,128)}, u32[]{:S(2)}) copy-start(f32[320,512]{1,0:T(8,128)} %get-tuple-element.66) | copy-start | bytes 1966084
  204.0 4.9 %copy-start.4 = (f32[320,512]{1,0:T(8,128)S(1)}, f32[320,512]{1,0:T(8,128)}, u32[]{:S(2)}) copy-start(f32[320,512]{1,0:T(8,128)} %get-tuple-element.20) | copy-start | bytes 1966084

commit v4 on v3

--- a/solution.py
+++ b/solution.py
@@ -77,6 +77,59 @@
             )
 
     pl.semaphore_wait(barrier, sum(jnp.where(here, 1, 0) for _, _, here in peers))
+
+
+def gather_kernel(hidden, cotangent, full_hidden, full_cotangent, send, recv):
+    tp = lax.axis_index("tp")
+    high, low = tp // 2, lax.rem(tp, 2)
+    near, far = tp + 1 - 2 * low, tp + 2 - 4 * high
+    width = hidden.shape[1]
+    always = tp >= 0
+    greet(pltpu.get_barrier_semaphore(), [("tp", near, always), ("tp", far, always)])
+    pairs = ((hidden, full_hidden), (cotangent, full_cotangent))
+
+    def columns(index):
+        return pl.ds(pl.multiple_of(index * width, width), width)
+
+    def copy(i, kind):
+        block, full = pairs[i]
+        mine = full.at[:, columns(tp)]
+        if kind == 2:
+            mine = full.at[:, columns(far)]
+            return remote(mine, mine, send.at[kind, i], recv.at[kind, i], "tp", near)
+        return remote(
+            block, mine, send.at[kind, i], recv.at[kind, i], "tp", far if kind == 0 else near
+        )
+
+    for kind in range(2):
+        for i in range(2):
+            copy(i, kind).start()
+    for block, full in pairs:
+        full[:, columns(tp)] = block[...]
+    for i in range(2):
+        copy(i, 0).wait_recv()
+        copy(i, 2).start()
+    for i in range(2):
+        copy(i, 1).wait_recv()
+        copy(i, 2).wait_recv()
+        for kind in range(3):
+            copy(i, kind).wait_send()
+
+
+def gather_both(hidden, cotangent):
+    rows, width = hidden.shape
+    full = jax.ShapeDtypeStruct((rows, width * lax.axis_size("tp")), BF16)
+    vmem = pl.BlockSpec(memory_space=pltpu.VMEM)
+    return pl.pallas_call(
+        gather_kernel,
+        out_shape=[full, full],
+        in_specs=[vmem] * 2,
+        out_specs=[vmem] * 2,
+        scratch_shapes=[pltpu.SemaphoreType.DMA((3, 2)), pltpu.SemaphoreType.DMA((3, 2))],
+        compiler_params=pltpu.CompilerParams(
+            collective_id=2, has_side_effects=True, vmem_limit_bytes=16 * 2**20
+        ),
+    )(hidden, cotangent)
 
 
 def tail_kernel(
@@ -177,7 +230,7 @@
 
     def product(c, base, left, slot):
         def body(b, carry):
-            parts[c, b] = (base[b] + dot(left[b], near_data[slot])).astype(BF16)
+            parts[c, b] = (base[b].astype(F32) + dot(left[b], near_data[slot])).astype(BF16)
             return carry
 
         lax.fori_loop(0, levels, body, 0)
@@ -216,7 +269,8 @@
     def term_body(i, carry):
         rows = pl.ds(pl.multiple_of(i * width, width), width)
         term[:, columns(i)] = (
-            term_base[:, columns(i)] + right_transposed_dot(kv_grad[...], kv_weights[rows, :])
+            term_base[:, columns(i)].astype(F32)
+            + right_transposed_dot(kv_grad[...], kv_weights[rows, :])
         ).astype(BF16)
         return carry
 
@@ -325,7 +379,7 @@
             three, three, some, some, sems, sems, sems, sems, three, three,
         ],
         compiler_params=pltpu.CompilerParams(
-            collective_id=1, has_side_effects=True, vmem_limit_bytes=56 * 2**20
+            collective_id=1, has_side_effects=True, vmem_limit_bytes=48 * 2**20
         ),
     )(attention, query_grad, kv_own, halo, own_t, near_t, cot_near_t, out_base, query_base,
       term_base, kv_weights)
@@ -350,11 +404,10 @@
         odd = split[:, :, 1].reshape(tok_rows, -1)
         return jnp.where(parity == 0, odd, even)
 
-    full_hidden = gather_features(hidden_in)
+    full_hidden, full_cotangent = gather_both(hidden_in, out_cotangent)
     kv_weights = jnp.concatenate([key_projection, value_projection], 1)
     key_values = dot(full_hidden, kv_weights).astype(BF16)
     halo = [shift(key_values, offset) for offset in range(1, reach + 1)]
-    full_cotangent = gather_features(out_cotangent)
     query_matrix = dot(full_hidden, query_proj).astype(BF16)
     attention_gradient = right_transposed_dot(full_cotangent, output_proj).astype(BF16)
 
@@ -427,9 +480,9 @@
         own_rows(full_hidden.T),
         near_rows(hidden_near),
         near_rows(cot_near),
-        own_rows(transposed_dot(full_cotangent, attention)),
-        own_rows(transposed_dot(full_hidden, query_grad)),
-        right_transposed_dot(query_grad, query_proj),
+        own_rows(transposed_dot(full_cotangent, attention).astype(BF16)),
+        own_rows(transposed_dot(full_hidden, query_grad).astype(BF16)),
+        right_transposed_dot(query_grad, query_proj).astype(BF16),
         kv_weights,
     )
     return (

time: 210 us -> 203 us (0.967)
  waiting for transfers between devices: 28.4 us -> 2.48 us
  Pallas kernels: 108 us -> 132 us
  other arithmetic: 21.3 us -> 15.2 us
  starting transfers between devices: 16.8 us -> 13 us
  matrix products: 21.5 us -> 24.7 us
    pallas_call x0 -> x1, Pallas kernels: none -> 34.2 us  [gather_both(): pl.pallas_call(gather_kernel, out_shape=[full, full], in_specs=[vmem] * 2...]
    ppermute x14 -> x8, waiting for transfers between devices: 28.4 us -> 2.48 us  [swap(): return lax.ppermute(value, axis, [(i, i ^ bit) for i in range(count)])]
    pallas_call x1, Pallas kernels: 108 us -> 98.3 us  [tail(): pl.pallas_call(functools.partial(tail_kernel, levels, count, reach), out_...]
    transpose x0 -> x1, local copies, waits for them, and re-layouts: none -> 4.5 us  [per_device(): output_grad, query_proj_grad, kv_proj_grad, hidden_grad = tail(attention,...]
    ppermute x14 -> x8, starting transfers between devices: 9.69 us -> 5.25 us  [swap(): return lax.ppermute(value, axis, [(i, i ^ bit) for i in range(count)])]
    dot_general x6, matrix products: 5.51 us -> 9.58 us  [dot(): return jnp.dot(left, right, preferred_element_type=F32)]
    select_n x4 -> x2, other arithmetic: 4.4 us -> 1.07 us  [gather_features(): first = jnp.where(high == 0, block, other)]
    unnamed x22 -> x32, local copies, waits for them, and re-layouts: 10.4 us -> 8.57 us
  transfers between devices with their start and end apart: 16 -> 10, of which waited for: 5 -> 4; matrix products, arithmetic and copies ran while one was open for 22% -> 21% of each run, Pallas kernels for 0% -> 0%
where the time goes in v4:
time: 203 us
  Pallas kernels  132 us (65%)
  matrix products  24.7 us (12%)
  other arithmetic  15.2 us (7%)
  local copies, waits for them, and re-layouts  14.1 us (7%)
  starting transfers between devices  13 us (6%)
  waiting for transfers between devices  2.48 us (1%)
    pallas_call x1, Pallas kernels, tail(): pl.pallas_call(functools.partial(tail_kernel, levels, count, reach), out_...  98.3 us
    pallas_call x1, Pallas kernels, gather_both(): pl.pallas_call(gather_kernel, out_shape=[full, full], in_specs=[vmem] * 2...  34.2 us
    dot_general x6, matrix products, dot(): return jnp.dot(left, right, preferred_element_type=F32)  9.58 us
    dot_general x6, matrix products, right_transposed_dot(): lax.dot_general(left, right, (((1,), (1,)), ((), ())), preferred_element_...  9.22 us
    unnamed x32, local copies, waits for them, and re-layouts  8.57 us
    ppermute x2, starting transfers between devices, shift(): lax.ppermute(value, 'seq', [(i, i + steps) for i in range(count) if 0 <=...  7.74 us
    dot_general x6, matrix products, transposed_dot(): lax.dot_general(left, right, (((0,), (0,)), ((), ())), preferred_element_...  5.86 us
    ppermute x8, starting transfers between devices, swap(): return lax.ppermute(value, axis, [(i, i ^ bit) for i in range(count)])  5.25 us
  transfers between devices with their start and end apart: 10, of which 4 were waited for; matrix products, arithmetic and copies ran while one was open for 21% of the time, Pallas kernels for 0%

profile of v4, /device:TPU:0, one launch (start us, length us, event | category | flops | bytes accessed | tf_op | source)
XLA Modules:
  0.0 202.9 jit_solution(18050241760242581612)
XLA Ops:
  0.7 1.6 constant_dynamic-update-slice_fusion.1
  2.5 34.2 %shard_map.110 = (bf16[512,2560]{1,0:T(8,128)(2,1)S(1)}, bf16[512,2560]{1,0:T(8,128)(2,1)S(1)}) custom-call(bf16[512,640]{1,0:T(8,128)(2,1)S(1)} %copy-done.3, bf16[512,640]{1,0:T(8,128)(2,1)S(1)} %copy-done.4), custom_call_target="tpu_custom_call" | custom-call | tf_op jit(solution)/shard_map/pallas_call | solution.py:123
  36.8 2.9 %convolution_convert_fusion.3 = bf16[512,512]{1,0:T(8,128)(2,1)} fusion(bf16[512,2560]{1,0:T(8,128)(2,1)S(1)} %get-tuple-element.15, bf16[2560,512]{1,0:T(8,128)(2,1)S(1)} %constant_dynamic-update-slice_fusion.kv_weights), kind=kOutput, calls=%fused_computation.44 | convolution fusion | flops 1342439424 | bytes 5767168 | tf_op jit(solution)/shard_map/dot_general | solution.py:18
  40.0 4.2 %collective-permute-start.3 = (bf16[512,512]{1,0:T(8,128)(2,1)}, bf16[512,512]{1,0:T(8,128)(2,1)}, u32[]{:S(2)}, u32[]{:S(2)}) collective-permute-start(bf16[512,512]{1,0:T(8,128)(2,1)} %convolution_convert_fusion.3), channel_id=1, source_target_pairs={{0,4},{4,8},{8,12},{12,16},{16,20},{20,24},{24,28},{1,5},{5,9},{9,... | collective-permute-start | bytes 1572872 | tf_op jit(solution)/shard_map/ppermute | solution.py:36
  44.2 3.5 %collective-permute-start.2 = (bf16[512,512]{1,0:T(8,128)(2,1)}, bf16[512,512]{1,0:T(8,128)(2,1)}, u32[]{:S(2)}, u32[]{:S(2)}) collective-permute-start(bf16[512,512]{1,0:T(8,128)(2,1)} %convolution_convert_fusion.3), channel_id=1, source_target_pairs={{0,8},{4,12},{8,16},{12,20},{16,24},{20,28},{1,9},{5,13},{9,17},{1... | collective-permute-start | bytes 1572872 | tf_op jit(solution)/shard_map/ppermute | solution.py:36
  47.7 1.1 copy.24
  48.8 1.8 fusion.28
  50.6 1.5 collective-permute-start
  52.2 1.3 copy.25
  53.5 0.8 fusion.27
  54.8 4.3 %convolution_convert_fusion.5 = bf16[512,512]{1,0:T(8,128)(2,1)} fusion(bf16[512,2560]{1,0:T(8,128)(2,1)} %copy-done.1, bf16[2560,512]{1,0:T(8,128)(2,1)S(1)} %copy-done), kind=kOutput, calls=%fused_computation.46 | convolution fusion | flops 1342439424 | bytes 5767168 | tf_op jit(solution)/shard_map/dot_general | solution.py:18
  59.1 1.5 convolution_convert_fusion.4
  60.7 4.5 %copy.34 = bf16[2560,512]{1,0:T(8,128)(2,1)} copy(bf16[2560,512]{0,1:T(8,128)(2,1)} %bitcast.74) | data formatting | bytes 5242880 | tf_op jit(solution)/shard_map/transpose | solution.py:480
  65.2 3.0 %fusion.17.own_t = bf16[4,320,512]{2,1,0:T(8,128)(2,1)} fusion(bf16[4,2,320,512]{3,2,1,0:T(8,128)(2,1)} %bitcast.76, pred[]{:T(512)S(6)} %eq.10), kind=kLoop, calls=%fused_computation.40 | loop fusion | flops 655360 | bytes 3932161 | tf_op jit(solution)/shard_map/jit(_where)/select_n | solution.py:470
  68.1 1.3 collective-permute-done.1
  69.4 1.1 collective-permute-start.4
  70.5 1.0 collective-permute-start.7
  71.5 1.5 pad_maximum_fusion.1
  73.0 1.2 fusion.40
  74.2 1.2 fusion.41
  75.5 0.6 fusion.11
  76.0 0.6 multiply_convert_fusion
  76.6 0.6 convolution_convert_fusion.8
  77.2 0.6 fusion.10
  77.8 0.6 multiply_convert_fusion.1
  78.3 0.7 multiply_reduce_fusion.1
  79.0 1.0 fusion.8
  80.1 0.6 convolution_convert_fusion.6
  80.7 0.6 fusion.29
  81.3 0.6 fusion.34
  81.9 1.1 fusion.9
  83.0 0.6 convolution_convert_fusion.7
  83.5 0.6 convolution_add_fusion.1
  84.2 0.6 convolution_add_fusion
  85.1 1.6 copy-done.2
  86.7 1.8 convolution_convert_fusion.1
  88.6 1.6 convolution_convert_fusion.2
  90.2 3.1 %convolution_convert_fusion.term_base = bf16[512,2560]{1,0:T(8,128)(2,1)} fusion(bf16[2560,512]{1,0:T(8,128)(2,1)S(1)} %copy-done, bf16[512,256]{1,0:T(8,128)(2,1)S(1)} %convolution_convert_fusion.6, bf16[512,256]{1,0:T(8,128)(2,1)S(1)} %convolution_convert_fusion.7), kind=kOutput, calls=%fused_computation | convolution fusion | flops 1344536576 | bytes 5767168 | tf_op jit(solution)/shard_map/dot_general | solution.py:26
  93.3 1.7 fusion.13
  95.1 1.0 broadcast_select_fusion.3
  96.3 0.6 collective-permute-start.5
  98.8 1.2 pad_maximum_fusion.2
  100.1 1.2 pad_maximum_fusion.3
  101.2 98.3 %shard_map.111 = (f32[320,512]{1,0:T(8,128)S(1)}, f32[320,512]{1,0:T(8,128)S(1)}, f32[320,512]{1,0:T(8,128)S(1)}, bf16[512,640]{1,0:T(8,128)(2,1)S(1)}) custom-call(bf16[512,512]{1,0:T(8,128)(2,1)S(1)} %get-tuple-element.50.attention, bf16[512,512]{1,0:T(8,128)(2,1)S(1)} %get-tuple-element.51.query_grad, f32[512,512]{1,0:T(8,128)S(1)} %fusion.18.kv_own, ...), custom_call_target="tpu_custom_call" | custom-call | tf_op jit(solution)/shard_map/pallas_call | solution.py:362
  199.5 0.9 fusion.39
  200.4 0.8 copy.59
  201.2 0.8 copy.60
  202.1 0.8 copy.61
  (53 shorter events, 3.7 us)
Async XLA Ops:
  0.6 54.1 %copy-start = (bf16[2560,512]{1,0:T(8,128)(2,1)S(1)}, bf16[2560,512]{1,0:T(8,128)(2,1)}, u32[]{:S(2)}) copy-start(bf16[2560,512]{1,0:T(8,128)(2,1)} %param.8) | copy-start | bytes 7864324
  0.6 1.6 copy-start.3
  0.7 1.8 copy-start.4
  0.7 36.0 %copy-start.9 = (bf16[2560,256]{1,0:T(8,128)(2,1)S(1)}, bf16[2560,256]{1,0:T(8,128)(2,1)}, u32[]{:S(2)}) copy-start(bf16[2560,256]{1,0:T(8,128)(2,1)} %param.10) | copy-start | bytes 3932164
  36.7 3.0 %copy-start.1 = (bf16[512,2560]{1,0:T(8,128)(2,1)}, bf16[512,2560]{1,0:T(8,128)(2,1)S(1)}, u32[]{:S(2)}) copy-start(bf16[512,2560]{1,0:T(8,128)(2,1)S(1)} %get-tuple-element.15) | copy-start | bytes 7864324
  36.7 3.0 %copy-start.5 = (bf16[512,2560]{1,0:T(8,128)(2,1)}, bf16[512,2560]{1,0:T(8,128)(2,1)S(1)}, u32[]{:S(2)}) copy-start(bf16[512,2560]{1,0:T(8,128)(2,1)S(1)} %get-tuple-element.16) | copy-start | bytes 7864324
  36.8 3.1 %copy-start.8 = (bf16[2560,512]{1,0:T(8,128)(2,1)}, bf16[2560,512]{1,0:T(8,128)(2,1)S(1)}, u32[]{:S(2)}) copy-start(bf16[2560,512]{1,0:T(8,128)(2,1)S(1)} %constant_dynamic-update-slice_fusion.kv_weights) | copy-start | bytes 7864324
  40.0 31.5 %collective-permute-start.3 = (bf16[512,512]{1,0:T(8,128)(2,1)}, bf16[512,512]{1,0:T(8,128)(2,1)}, u32[]{:S(2)}, u32[]{:S(2)}) collective-permute-start(bf16[512,512]{1,0:T(8,128)(2,1)} %convolution_convert_fusion.3), channel_id=1, source_target_pairs={{0,4},{4,8},{8,12},{12,16},{16,20},{20,24},{24,28},{1,5},{5,9},{9,... | collective-permute-start | bytes 1572872 | tf_op jit(solution)/shard_map/ppermute | solution.py:36
  44.2 27.3 %collective-permute-start.2 = (bf16[512,512]{1,0:T(8,128)(2,1)}, bf16[512,512]{1,0:T(8,128)(2,1)}, u32[]{:S(2)}, u32[]{:S(2)}) collective-permute-start(bf16[512,512]{1,0:T(8,128)(2,1)} %convolution_convert_fusion.3), channel_id=1, source_target_pairs={{0,8},{4,12},{8,16},{12,20},{16,24},{20,28},{1,9},{5,13},{9,17},{1... | collective-permute-start | bytes 1572872 | tf_op jit(solution)/shard_map/ppermute | solution.py:36
  50.6 17.5 %collective-permute-start = (bf16[512,320]{0,1:T(8,128)(2,1)}, bf16[512,320]{0,1:T(8,128)(2,1)}, u32[]{:S(2)}, u32[]{:S(2)}) collective-permute-start(bf16[512,320]{0,1:T(8,128)(2,1)} %fusion.28), channel_id=1, source_target_pairs={{0,4},{4,0},{8,12},{12,8},{16,20},{20,16},{24,28},{28,24},{1,5},{5... | collective-permute-start | bytes 983048 | tf_op jit(solution)/shard_map/ppermute | solution.py:31
  54.2 4.8 %copy-start.6 = (bf16[512,2560]{1,0:T(8,128)(2,1)S(1)}, bf16[512,2560]{1,0:T(8,128)(2,1)}, u32[]{:S(2)}) copy-start(bf16[512,2560]{1,0:T(8,128)(2,1)} %copy-done.5) | copy-start | bytes 7864324
  54.2 4.8 %copy-start.11 = (bf16[512,2560]{1,0:T(8,128)(2,1)S(1)}, bf16[512,2560]{1,0:T(8,128)(2,1)}, u32[]{:S(2)}) copy-start(bf16[512,2560]{1,0:T(8,128)(2,1)} %param.11) | copy-start | bytes 7864324
  54.3 15.2 %collective-permute-start.1 = (bf16[512,320]{0,1:T(8,128)(2,1)}, bf16[512,320]{0,1:T(8,128)(2,1)S(1)}, u32[]{:S(2)}, u32[]{:S(2)}) collective-permute-start(bf16[512,320]{0,1:T(8,128)(2,1)} %fusion.27), channel_id=1, source_target_pairs={{0,4},{4,0},{8,12},{12,8},{16,20},{20,16},{24,28},{28,24},{1,5},{5... | collective-permute-start | bytes 983048 | tf_op jit(solution)/shard_map/ppermute | solution.py:31
  65.2 7.8 %copy-start.10 = (bf16[512,512]{1,0:T(8,128)(2,1)S(1)}, bf16[512,512]{1,0:T(8,128)(2,1)}, u32[]{:S(2)}) copy-start(bf16[512,512]{1,0:T(8,128)(2,1)} %convolution_convert_fusion.5) | copy-start | bytes 1572868
  65.2 7.8 %copy-start.12 = (s32[512]{0:T(512)S(1)}, s32[512]{0:T(512)}, u32[]{:S(2)}) copy-start(s32[512]{0:T(512)} %param.13) | copy-start | bytes 6148
  69.4 25.6 %collective-permute-start.4 = (bf16[512,320]{0,1:T(8,128)(2,1)}, bf16[512,320]{0,1:T(8,128)(2,1)S(1)}, u32[]{:S(2)}, u32[]{:S(2)}) collective-permute-start(bf16[512,320]{0,1:T(8,128)(2,1)} %collective-permute-done), channel_id=1, source_target_pairs={{0,2},{1,3},{2,0},{3,1},{4,6},{5,7},{6,4},{7,5},{8,10},{9,11},{10,... | collective-permute-start | bytes 983048 | tf_op jit(solution)/shard_map/ppermute | solution.py:31
  70.5 26.3 %collective-permute-start.7 = (bf16[512,320]{0,1:T(8,128)(2,1)S(1)}, bf16[512,320]{0,1:T(8,128)(2,1)S(1)}, u32[]{:S(2)}, u32[]{:S(2)}) collective-permute-start(bf16[512,320]{0,1:T(8,128)(2,1)S(1)} %collective-permute-done.1), channel_id=1, source_target_pairs={{0,2},{1,3},{2,0},{3,1},{4,6},{5,7},{6,4},{7,5},{8,10},{9,11},{10,... | collective-permute-start | bytes 983048 | tf_op jit(solution)/shard_map/ppermute | solution.py:31
  85.0 1.7 copy-start.2
  86.7 1.9 copy-start.7
  96.1 1.7 collective-permute-start.6
  96.3 2.0 collective-permute-start.5
  96.9 1.8 collective-permute-start.9
  97.0 3.0 %collective-permute-start.8 = (bf16[512,320]{0,1:T(8,128)(2,1)S(1)}, bf16[512,320]{0,1:T(8,128)(2,1)S(1)}, u32[]{:S(2)}, u32[]{:S(2)}) collective-permute-start(bf16[512,320]{0,1:T(8,128)(2,1)S(1)} %get-tuple-element.33), channel_id=1, source_target_pairs={{0,1},{1,0},{2,3},{3,2},{4,5},{5,4},{6,7},{7,6},{8,9},{9,8},{10,11... | collective-permute-start | bytes 983048 | tf_op jit(solution)/shard_map/ppermute | solution.py:31
